TPU v7x, 256 devices: a whole 4x4x8 slice. The times are simulated.
256 devices in a mesh: ctx: 32 (over z, x_hi, core), head: 8 (over x_lo, y).
Axes of the slice: x: 4 (x_hi: 2, x_lo: 2; x = x_hi * 2 + x_lo), y: 4, z: 8, core: 2. Of those that a mesh axis runs over, the one named last changes fastest.
Arguments:
- queries: bfloat16 [4096, 12288], P('ctx', 'head'), may hold values from -256 to 256
- latent_rope: bfloat16 [4096, 576], P('ctx'), may hold values from -8 to 8
- key_up: bfloat16 [512, 8192], P(None, 'head'), may hold values from -0.25 to 0.25
- value_up: bfloat16 [512, 8192], P(None, 'head'), may hold values from -0.25 to 0.25
- out_weight: bfloat16 [8192, 7168], P('head', 'ctx'), may hold values from -1 to 1
- plan: int32 [32, 2], replicated, may hold values from 0 to 63, as said below
Outputs:
- mixed: bfloat16 [4096, 7168], P('ctx', 'head')
Inputs may be any that keep to these rules, and one draw needn't show every extreme that they name: `plan`: row c names the two blocks of 64 consecutive positions held by device c of ctx, in the order of its rows; the two add up to 63, and every block appears once.
All inputs are finite; a program needn't handle non-finite values.
Results may differ from a plain program's by a relative error of at most 0.018.
Values may be sent and summed in bfloat16 or wider, within the bound.
A program may use at most 128 MiB of HBM per device.

v0:
```python
import jax
import jax.numpy as jnp
from jax import lax
from jax.sharding import PartitionSpec as P

NOPE = 128
ROPE = 64
VDIM = 128
LATENT = 512


big_negative = -1e30


def block_positions(plan, first_row, row_total, shard_rows):
    flat_table = plan.reshape(-1)
    half_rows = shard_rows // 2
    global_rows = first_row + jnp.arange(row_total, dtype=jnp.int32)
    slot_index = global_rows // shard_rows * 2 + global_rows % shard_rows // half_rows
    matches = slot_index[:, None] == jnp.arange(flat_table.shape[0], dtype=jnp.int32)[None, :]
    block_ids = jnp.sum(jnp.where(matches, flat_table[None, :], 0), axis=1)
    return block_ids * half_rows + global_rows % half_rows


def attend(
    carried,
    query_nope,
    query_rope,
    query_pos,
    key_rows,
    value_rows,
    rope_rows,
    key_pos,
    score_scale,
):
    run_max, run_sum, run_out = carried
    scores = jnp.einsum("qhd,khd->hqk", query_nope, key_rows, preferred_element_type=jnp.float32)
    scores = scores + jnp.einsum(
        "qhd,kd->hqk", query_rope, rope_rows, preferred_element_type=jnp.float32
    )
    scores = scores * score_scale
    allowed = (query_pos[:, None] >= key_pos[None, :])[None, :, :]
    scores = jnp.where(allowed, scores, big_negative)
    new_max = jnp.maximum(run_max, jnp.max(scores, axis=2))
    weights = jnp.where(allowed, jnp.exp(scores - new_max[:, :, None]), 0.0)
    run_sum = jnp.sum(weights, axis=2)
    added = jnp.einsum(
        "hqk,khd->hqd", weights.astype(jnp.bfloat16), value_rows, preferred_element_type=jnp.float32
    )
    run_out = added
    return (new_max, run_sum, run_out)


def body(queries, latent_rope, key_up, value_up, out_weight, plan):
    row_count = queries.shape[0]
    head_count = key_up.shape[1] // NOPE
    my_index = lax.axis_index("ctx")
    query_all = queries.reshape(row_count, head_count, NOPE + ROPE)
    query_nope = query_all[:, :, :NOPE]
    query_rope = query_all[:, :, NOPE:]
    query_pos = block_positions(plan, my_index * row_count, row_count, row_count)
    score_scale = (NOPE + ROPE) ** (-0.5)
    initial = (
        jnp.full((head_count, row_count), big_negative, jnp.float32),
        jnp.zeros((head_count, row_count), jnp.float32),
        jnp.zeros((head_count, row_count, VDIM), jnp.float32),
    )
    latent_part = lax.all_gather(latent_rope, "ctx", axis=0, tiled=True)
    latent_only = latent_part[:, :LATENT]
    key_rows = jnp.dot(latent_only, key_up, preferred_element_type=jnp.float32).astype(jnp.bfloat16)
    value_rows = jnp.dot(latent_only, value_up, preferred_element_type=jnp.float32).astype(
        jnp.bfloat16
    )
    key_rows, value_rows, rope_rows = (key_rows, value_rows, latent_part[:, LATENT:])
    count_here = key_rows.shape[0]
    key_pos = block_positions(plan, jnp.int32(0), count_here, row_count)
    run_max, run_sum, run_out = attend(
        initial,
        query_nope,
        query_rope,
        query_pos,
        key_rows.reshape(count_here, head_count, NOPE),
        value_rows.reshape(count_here, head_count, VDIM),
        rope_rows,
        key_pos,
        score_scale,
    )
    per_head = (run_out / run_sum[:, :, None]).astype(jnp.bfloat16)
    attended = jnp.transpose(per_head, (1, 0, 2)).reshape(row_count, head_count * VDIM)
    head_partial = jnp.dot(
        attended,
        lax.all_gather(out_weight, "ctx", axis=1, tiled=True),
        preferred_element_type=jnp.float32,
    )
    mixed = lax.psum_scatter(
        head_partial.astype(jnp.bfloat16), "head", scatter_dimension=1, tiled=True
    )
    return mixed


def solution(mesh):
    placed = (
        P("ctx", "head"),
        P("ctx", None),
        P(None, "head"),
        P(None, "head"),
        P("head", "ctx"),
        P(),
    )
    return jax.shard_map(
        body, mesh=mesh, in_specs=placed, out_specs=P("ctx", "head"), check_vma=False
    )
```

profile of v0, /device:TPU:1, one launch (start us, length us, event | category | flops | bytes accessed | tf_op | source)
XLA Modules:
  0.0 286.9 jit_solution(16563333637440184050)
XLA Ops:
  6.5 0.0 copy-start
  6.5 0.0 all-gather.3.cloned.1.call-start
  6.5 0.7 all-gather.3.cloned.1.call-update
  7.3 0.0 all-gather.5.cloned.1.call-start
  7.3 0.7 all-gather.5.cloned.1.call-update
  8.0 0.0 reduce-scatter.4.cloned.1.call-start
  8.1 0.8 copy.21
  8.8 0.1 broadcast_in_dim.56
  8.9 1.2 copy.22
  10.2 0.1 select_reduce_fusion.1
  10.3 0.2 select_reduce_fusion
  10.6 1.9 broadcast_compare_fusion
  12.4 91.4 %all-gather.3.cloned.1.call-done = bf16[4096,576]{0,1:T(8,128)(2,1)} async-done(((bf16[128,576]{0,1:T(8,128)(2,1)}), bf16[4096,576]{0,1:T(8,128)(2,1)}) %all-gather.3.cloned.1.call-update) | async-done | bytes 4718608 | tf_op jit(solution)/shard_map/all_gather | solution.py:68
  103.8 0.0 copy-done
  103.8 8.9 %convolution_convert_fusion.2 = bf16[4096,1024]{0,1:T(8,128)(2,1)} fusion(bf16[512,1024]{1,0:T(8,128)(2,1)S(1)} %copy-done, bf16[4096,576]{0,1:T(8,128)(2,1)} %all-gather.3.cloned.1.call-done), kind=kOutput, calls=%fused_computation.12 | convolution fusion | flops 4299161600 | bytes 13631488 | tf_op jit(solution)/shard_map/dot_general | solution.py:70
  112.8 12.0 %fusion.20 = f32[8,4096,128]{2,1,0:T(8,128)} fusion(bf16[4096,8,128]{0,2,1:T(8,128)(2,1)} %bitcast.32, bf16[128,8,192]{0,2,1:T(8,128)(2,1)S(1)} %bitcast.34), kind=kOutput, calls=%fused_computation.22 | convolution fusion | flops 1073741824 | bytes 25427968 | tf_op jit(solution)/shard_map/qhd,khd->hqk/dot_general | solution.py:37
  124.8 10.9 %fusion.44 = (f32[8,128]{1,0:T(8,128)S(1)}, f32[8,128,4096]{1,2,0:T(8,128)}) fusion(bf16[128,8,192]{0,2,1:T(8,128)(2,1)S(1)} %bitcast.35, bf16[4096,576]{0,1:T(8,128)(2,1)} %all-gather.3.cloned.1.call-done, f32[8,4096,128]{2,1,0:T(8,128)} %fusion.20, pred[128,4096]{0,1:T(8,128)(4,1)S(1)} %broadcast_compare_fusion), kind=kOutput, calls=%fused_computation.71 | convolution fusion | flops 553647104 | bytes 34738176 | tf_op jit(solution)/shard_map/qhd,kd->hqk/dot_general | solution.py:38
  135.7 0.0 copy-start.2
  135.7 8.9 %fusion.2 = f32[8,128]{1,0:T(8,128)S(1)} fusion(f32[8,128,4096]{1,2,0:T(8,128)} %get-tuple-element.6, f32[8,128]{1,0:T(8,128)S(1)} %broadcast_maximum_fusion, pred[128,4096]{0,1:T(8,128)(4,1)S(1)} %broadcast_compare_fusion), kind=kLoop, calls=%fused_computation.4 | loop fusion | flops 12581888 | bytes 17309696 | tf_op jit(solution)/shard_map/reduce_sum | solution.py:46
  144.6 0.0 copy-done.2
  144.6 9.1 %convolution_convert_fusion.1 = bf16[4096,1024]{0,1:T(8,128)(2,1)} fusion(bf16[512,1024]{1,0:T(8,128)(2,1)S(1)} %copy-done.2, bf16[4096,576]{0,1:T(8,128)(2,1)} %all-gather.3.cloned.1.call-done), kind=kOutput, calls=%fused_computation.11 | convolution fusion | flops 4299161600 | bytes 13631488 | tf_op jit(solution)/shard_map/dot_general | solution.py:71
  153.7 13.5 %fusion.17 = bf16[128,8,128]{0,2,1:T(8,128)(2,1)S(1)} fusion(bf16[4096,8,128]{0,2,1:T(8,128)(2,1)} %bitcast.39, f32[8,128,4096]{1,2,0:T(8,128)} %get-tuple-element.6, f32[8,128]{1,0:T(8,128)S(1)} %broadcast_maximum_fusion, pred[128,4096]{0,1:T(8,128)(4,1)S(1)} %broadcast_compare_fusion, f32[128,8]{0,1:T(8,128)S(1)} %bitcast.38), kind=kOutput, calls=%fused_computation.20 | convolution fusion | flops 1086586880 | bytes 25960448 | tf_op jit(solution)/shard_map/hqk,khd->hqd/dot_general | solution.py:47
  167.3 63.3 %all-gather.5.cloned.1.call-done = bf16[1024,7168]{0,1:T(8,128)(2,1)} async-done(((bf16[1024,224]{0,1:T(8,128)(2,1)}), bf16[1024,7168]{0,1:T(8,128)(2,1)}) %all-gather.5.cloned.1.call-update) | async-done | bytes 14680080 | tf_op jit(solution)/shard_map/all_gather | solution.py:92
  230.6 0.0 copy-start.1
  230.6 10.2 %convolution_convert_fusion = bf16[128,7168]{1,0:T(8,128)(2,1)S(1)} fusion(bf16[128,1024]{0,1:T(8,128)(2,1)S(1)} %bitcast.36, bf16[1024,7168]{0,1:T(8,128)(2,1)} %all-gather.5.cloned.1.call-done), kind=kOutput, calls=%fused_computation.6 | convolution fusion | flops 1879965696 | bytes 16777216 | tf_op jit(solution)/shard_map/dot_general | solution.py:90
  240.8 2.3 copy.28
  243.2 0.0 reduce-scatter.4.cloned.1.call-update
  243.2 35.4 %reduce-scatter.4.cloned.1.call-done = bf16[896,128]{1,0:T(8,128)(2,1)} async-done(((bf16[7168,128]{1,0:T(8,128)(2,1)}), bf16[896,128]{1,0:T(8,128)(2,1)}) %reduce-scatter.4.cloned.1.call-update) | async-done | bytes 229392
  278.6 1.8 copy.29
  280.3 0.0 copy-done.1
  (5 shorter events, 0.1 us)
Async XLA Ops:
  6.5 97.3 %copy-start = (bf16[512,1024]{1,0:T(8,128)(2,1)S(1)}, bf16[512,1024]{1,0:T(8,128)(2,1)}, u32[]{:S(2)}) copy-start(bf16[512,1024]{1,0:T(8,128)(2,1)} %param.8) | copy-start | bytes 3145732
  6.5 97.3 %all-gather.3.cloned.1.call-start = ((), (), s32[]{:S(2)}) async-start(), calls=%async_computation.1 | async-start | bytes 4866048 | tf_op jit(solution)/shard_map/all_gather | solution.py:68
  7.3 223.3 %all-gather.5.cloned.1.call-start = ((), (), s32[]{:S(2)}) async-start(), calls=%async_computation.2 | async-start | bytes 15138816 | tf_op jit(solution)/shard_map/all_gather | solution.py:92
  8.0 270.6 %reduce-scatter.4.cloned.1.call-start = ((), (), s32[]{:S(2)}) async-start(), calls=%async_computation.3 | async-start | bytes 2064384
  135.7 8.9 %copy-start.2 = (bf16[512,1024]{1,0:T(8,128)(2,1)S(1)}, bf16[512,1024]{1,0:T(8,128)(2,1)}, u32[]{:S(2)}) copy-start(bf16[512,1024]{1,0:T(8,128)(2,1)} %param.9) | copy-start | bytes 3145732
  230.6 49.7 %copy-start.1 = (bf16[512,1024]{1,0:T(8,128)(2,1)S(1)}, bf16[512,1024]{1,0:T(8,128)(2,1)}, u32[]{:S(2)}) copy-start(bf16[512,1024]{1,0:T(8,128)(2,1)} %param.8) | copy-start | bytes 3145732
Sparse Core Ops, SparseCore 0:
  9.9 93.8 all-gather.2
  106.6 123.9 all-gather.4
  243.3 35.2 reduce-scatter.3
where the time goes:
time: 291 us; the launch traced here: 287 us
  waiting for transfers between devices  192 us (66%)
  matrix products  64.7 us (22%)
  between operations  13.2 us (5%)
  other arithmetic  11.1 us (4%)
  local copies, waits for them, and re-layouts  6.19 us (2%)
    all_gather x1, waiting for transfers between devices, body(): latent_part = lax.all_gather(latent_rope, 'ctx', axis=0, tiled=True)  91.4 us
    all_gather x1, waiting for transfers between devices, body(): lax.all_gather(out_weight, 'ctx', axis=1, tiled=True)  63.3 us
    unnamed x4, waiting for transfers between devices  36.8 us
    dot_general x1, matrix products, attend(): jnp.einsum('hqk,khd->hqd', weights.astype(jnp.bfloat16), value_rows, pref...  13.5 us
    dot_general x1, matrix products, attend(): jnp.einsum('qhd,khd->hqk', query_nope, key_rows, preferred_element_type=j...  12 us
    dot_general x1, matrix products, attend(): jnp.einsum('qhd,kd->hqk', query_rope, rope_rows, preferred_element_type=j...  10.9 us
    dot_general x1, matrix products, body(): jnp.dot(attended, lax.all_gather(out_weight, 'ctx', axis=1, tiled=True),...  10.2 us
    dot_general x1, matrix products, body(): jnp.dot(latent_only, value_up, preferred_element_type=jnp.float32)  9.14 us
  transfers between devices with their start and end apart: 3, of which 3 were waited for; matrix products, arithmetic and copies ran while one was open for 24% of the time, Pallas kernels for 0%

commit v1 on v0

v1 whole, which is shorter than its diff:
```python
import functools

import jax
import jax.numpy as jnp
from jax import lax
from jax.experimental import pallas as pl
from jax.experimental.pallas import tpu as pltpu
from jax.sharding import PartitionSpec as P

MESH = pl.DeviceIdType.MESH
NOPE = 128
ROPE = 64
VDIM = 128
LATENT = 512
HEAD_LOCAL = 8
GROUP = 4
BLOCK = 64
TASKS = 17
WIDE = 640
NEG = -1e30
SCALE2 = 1.4426950408889634 * (NOPE + ROPE) ** -0.5


def nt(a, b):
    return lax.dot_general(a, b, (((1,), (1,)), ((), ())), preferred_element_type=jnp.float32)


def kernel(
    plan_ref, inv_ref, q_ref, lr_ref, ku_ref, vu_ref, w_ref, out_ref,
    lat, qs, sbuf, mrun, mfin, lrun, acc, wt, wbuf, att, csend, crecv, fsend, frecv,
    zs, zr, xs, xr, ys, yr, ks, kr, w0, ws, wr, as_, ar, bs, br, cs, cr, fs, fr,
):
    ctx = lax.axis_index("ctx")
    head = lax.axis_index("head")
    core = lax.rem(ctx, 2)
    xh = lax.rem(ctx // 2, 2)
    z = ctx // 4
    xl = head // 4
    y = lax.rem(head, 4)
    x = xh * 2 + xl

    def dev(z_, x_, y_, c_):
        return ((z_ * 2 + x_ // 2) * 2 + c_, lax.rem(x_, 2) * 4 + y_)

    def zdev(d):
        return dev(lax.rem(z + d, 8), x, y, core)

    def xdev(o):
        return dev(z, lax.rem(x + o, 4), y, core)

    def ydev(o):
        return dev(z, x, lax.rem(y + o, 4), core)

    other = dev(z, x, y, 1 - core)

    def rcopy(src, dst, ssem, rsem, target):
        return pltpu.make_async_remote_copy(
            src_ref=src, dst_ref=dst, send_sem=ssem, recv_sem=rsem,
            device_id=target, device_id_type=MESH,
        )

    barrier = pltpu.get_barrier_semaphore()
    for d in range(1, 8):
        pl.semaphore_signal(barrier, 1, device_id=zdev(d), device_id_type=MESH)
    for o in range(1, 4):
        pl.semaphore_signal(barrier, 1, device_id=ydev(o), device_id_type=MESH)
    for o in range(4):
        if o:
            pl.semaphore_signal(barrier, 1, device_id=xdev(o), device_id_type=MESH)
        pl.semaphore_signal(
            barrier, 1, device_id=dev(z, lax.rem(x + o, 4), y, 1 - core), device_id_type=MESH
        )

    par = lax.rem(y, 2)

    def piece(src_x, parity, c_):
        return (src_x // 2) * 8 + c_ * 4 + parity * 2 + lax.rem(src_x, 2)

    mine = piece(x, par, core)
    block = lr_ref[pl.ds((par * 2 + xl) * 32, 32), :]
    lat[z, mine, :, 0:LATENT] = block[:, :LATENT]
    lat[z, mine, :, LATENT:WIDE] = jnp.concatenate(
        [block[:, LATENT:], jnp.zeros((32, WIDE - LATENT - ROPE), jnp.bfloat16)], axis=1
    )
    pl.semaphore_wait(barrier, 17)

    zcopies = []
    for d in range(1, 8):
        cp = rcopy(lat.at[z, mine], lat.at[z, mine], zs.at[d - 1], zr.at[d - 1], zdev(d))
        cp.start()
        zcopies.append(cp)

    wt[...] = jnp.transpose(w_ref[...], (1, 0))
    wj = lax.rem(z, 4)
    keeper = z // 4
    at_home = jnp.logical_and(core == xl, core == keeper)

    @pl.when(at_home)
    def _():
        pltpu.make_async_copy(wt, wbuf.at[wj, xl], wr.at[wj, xl]).start()

    @pl.when(jnp.logical_not(at_home))
    def _():
        rcopy(
            wt, wbuf.at[wj, xl], w0.at[0], wr.at[wj, xl], dev(z, xh * 2 + core, y, keeper)
        ).start()

    for h in range(HEAD_LOCAL):
        lo = h * (NOPE + ROPE)
        qn = q_ref[:, lo : lo + NOPE]
        qr = q_ref[:, lo + NOPE : lo + NOPE + ROPE]
        ql = nt(qn, ku_ref[:, h * NOPE : (h + 1) * NOPE]).astype(jnp.bfloat16)
        qr = jnp.concatenate([qr, jnp.zeros((2 * BLOCK, WIDE - LATENT - ROPE), jnp.bfloat16)], axis=1)
        g, r = h // GROUP, (h % GROUP) * BLOCK
        for i in range(2):
            qs[g, i, r : r + BLOCK, 0:LATENT] = ql[i * BLOCK : (i + 1) * BLOCK]
            qs[g, i, r : r + BLOCK, LATENT:WIDE] = qr[i * BLOCK : (i + 1) * BLOCK]

    for cp in zcopies:
        cp.wait()

    pending = []

    def region(idx):
        return lat.at[pl.ds(0, 8), idx]

    def half(idx, hz):
        return lat.at[pl.ds(4 * hz, 4), idx]

    def spread(o):
        src_x = lax.rem(x + 4 - o, 4)
        idx = piece(src_x, par, core)
        for n in range(2):
            cp = rcopy(half(idx, n), half(idx, n), ys.at[o, n], yr.at[o, n], ydev(1 + 2 * n))
            cp.start()
            pending.append(cp)
        cp = rcopy(region(idx), region(idx), ks.at[o, 0], kr.at[o, 0], other)
        cp.start()
        pending.append(cp)

    def ring_send(j, part, up):
        slot = wbuf.at[j, part]
        n = 0 if up else 1
        rcopy(slot, slot, ws.at[n, j, part], wr.at[j, part], zdev(1 if up else 7)).start()

    def ring_wait(j, part):
        slot = wbuf.at[j, part]
        rcopy(slot, slot, w0.at[0], wr.at[j, part], other).wait_recv()

    def ring_step(s):
        if s == 0:
            @pl.when(core == keeper)
            def _():
                for part in range(2):
                    ring_wait(wj, part)
                for part in range(2):
                    ring_send(wj, part, True)
                    ring_send(wj, part, False)
            return
        for up in (True, False):
            zsrc = lax.rem(z + (8 - s if up else s), 8)
            j = lax.rem(zsrc, 4)

            @pl.when(core == zsrc // 4)
            def _():
                far = 0 if up else 1
                if s <= 4:
                    ring_wait(j, far)
                if s <= 3:
                    ring_wait(j, 1 - far)
                if s < 4:
                    ring_send(j, far, up)
                if s < 3:
                    ring_send(j, 1 - far, up)

    xcopies = []
    for o in (1, 3, 2):
        cp = rcopy(region(mine), region(mine), xs.at[o - 1], xr.at[o - 1], xdev(o))
        cp.start()
        xcopies.append((o, cp))
    spread(0)
    ring_step(0)
    for o, cp in xcopies:
        cp.wait()
        spread(o)
    ycopies = []
    for o in (0, 1, 3, 2):
        src_x = lax.rem(x + 4 - o, 4)
        idx = piece(src_x, 1 - par, core)
        for n in range(2):
            rcopy(half(idx, n), half(idx, n), ys.at[o, n], yr.at[o, n], other).wait_recv()
        cp = rcopy(region(idx), region(idx), ks.at[o, 1], kr.at[o, 1], other)
        cp.start()
        ycopies.append(cp)
    for cp in pending:
        cp.wait_send()
    for o in range(4):
        src_x = lax.rem(x + 4 - o, 4)
        for n, parity in ((0, par), (1, 1 - par)):
            idx = piece(src_x, parity, 1 - core)
            rcopy(region(idx), region(idx), ks.at[o, n], kr.at[o, n], other).wait_recv()
    for cp in ycopies:
        cp.wait_send()

    p0 = plan_ref[ctx, 0]
    p1 = plan_ref[ctx, 1]
    low = jnp.minimum(p0, p1)
    high = jnp.maximum(p0, p1)
    low_at = jnp.where(p0 < p1, 0, 1)
    beta = lax.div(low, 4)
    rows = GROUP * BLOCK
    row_of = lax.broadcasted_iota(jnp.int32, (rows, 256), 0) % BLOCK
    lane_of = lax.broadcasted_iota(jnp.int32, (rows, 256), 1)
    ahead = lane_of - row_of

    def chunk_of(t):
        return jnp.where(t <= beta, t, t - beta - 1)

    def keys_of(t):
        first = chunk_of(t) * 4
        got = []
        for i in range(4):
            s = inv_ref[first + i]
            got.append(lat[lax.div(s, 8), pl.ds(lax.rem(s, 8) * 2, 2)].reshape(BLOCK, WIDE))
        return jnp.concatenate(got, axis=0)

    for g in range(2):
        mrun[0] = jnp.full((rows, 128), NEG, jnp.float32)
        lrun[0] = jnp.zeros((rows, 128), jnp.float32)
        acc[0] = jnp.zeros((rows, LATENT), jnp.float32)

        def score(t, carry):
            is_low = t <= beta
            q = qs[g, jnp.where(is_low, low_at, 1 - low_at)]
            s = nt(q, keys_of(t)) * SCALE2
            room = jnp.where(is_low, low, high) * BLOCK - chunk_of(t) * 256
            s = jnp.where(ahead <= room, s, NEG)
            sbuf[t] = s
            before = jnp.where(t == beta + 1, NEG, mrun[t])
            mrun[t + 1] = jnp.maximum(before, jnp.maximum(s[:, :128], s[:, 128:]))
            return carry

        lax.fori_loop(0, TASKS, score, 0)
        mfin[0] = jnp.broadcast_to(jnp.max(mrun[beta + 1], axis=1, keepdims=True), (rows, 128))
        mfin[1] = jnp.broadcast_to(jnp.max(mrun[TASKS], axis=1, keepdims=True), (rows, 128))

        def weigh(t, carry):
            is_low = t <= beta
            keep = jnp.where(t == beta + 1, 0.0, 1.0)
            m = mfin[jnp.where(is_low, 0, 1)]
            s = sbuf[t]
            wa = jnp.exp2(s[:, :128] - m)
            wb = jnp.exp2(s[:, 128:] - m)
            lrun[t + 1] = lrun[t] * keep + (wa + wb)
            w = jnp.concatenate([wa, wb], axis=1).astype(jnp.bfloat16)
            added = jnp.dot(w, keys_of(t)[:, :LATENT], preferred_element_type=jnp.float32)
            acc[t + 1] = acc[t] * keep + added
            return carry

        lax.fori_loop(0, TASKS, weigh, 0)

        def normal(at):
            total = jnp.sum(lrun[at], axis=1, keepdims=True)
            return (acc[at] / total).astype(jnp.bfloat16)

        o_low = normal(beta + 1)
        o_high = normal(TASKS)
        first = jnp.where(low_at == 0, o_low, o_high)
        second = jnp.where(low_at == 0, o_high, o_low)
        for hh in range(GROUP):
            h = g * GROUP + hh
            r = slice(hh * BLOCK, (hh + 1) * BLOCK)
            o = jnp.concatenate([first[r], second[r]], axis=0)
            up = jnp.dot(o, vu_ref[:, h * VDIM : (h + 1) * VDIM], preferred_element_type=jnp.float32)
            att[xl, xh, core, :, h * VDIM : (h + 1) * VDIM] = up.astype(jnp.bfloat16)

        def shard(src_x, c_):
            return att.at[
                lax.rem(src_x, 2), src_x // 2, c_, :, pl.ds(g * GROUP * VDIM, GROUP * VDIM)
            ]

        for o in (1, 3, 2):
            rcopy(shard(x, core), shard(x, core), as_.at[g, o - 1], ar.at[g, o - 1], xdev(o)).start()
        rcopy(shard(x, core), shard(x, core), bs.at[g, 0], br.at[g, 0], other).start()
        ring_step(g + 1)

    for g in range(2):
        def shard(src_x, c_):
            return att.at[
                lax.rem(src_x, 2), src_x // 2, c_, :, pl.ds(g * GROUP * VDIM, GROUP * VDIM)
            ]

        for o in (1, 3, 2):
            there = shard(lax.rem(x + 4 - o, 4), core)
            cp = rcopy(there, there, as_.at[g, o - 1], ar.at[g, o - 1], other)
            cp.wait_recv()
            cp.wait_send()
            rcopy(there, there, bs.at[g, o], br.at[g, o], other).start()
    for g in range(2):
        for o in range(4):
            def shard(src_x, c_):
                return att.at[
                    lax.rem(src_x, 2), src_x // 2, c_, :, pl.ds(g * GROUP * VDIM, GROUP * VDIM)
                ]

            there = shard(lax.rem(x + 4 - o, 4), 1 - core)
            cp = rcopy(there, there, bs.at[g, o], br.at[g, o], other)
            cp.wait_recv()
            cp.wait_send()

    def project(zsrc):
        j = lax.rem(zsrc, 4)

        @pl.when(core == zsrc // 4)
        def _():
            total = nt(wbuf[j, 0], att[0].reshape(512, 1024)) + nt(
                wbuf[j, 1], att[1].reshape(512, 1024)
            )
            csend[j] = total.astype(jnp.bfloat16)
            o = lax.rem(j + 4 - y, 4)

            @pl.when(o != 0)
            def _():
                rcopy(csend.at[j], crecv.at[o], cs.at[o], cr.at[o], dev(z, x, j, core)).start()

    def two(s, carry):
        project(lax.rem(z + 8 - s, 8))
        project(lax.rem(z + s, 8))
        return carry

    project(z)
    lax.fori_loop(1, 3, two, 0)
    ring_step(3)
    lax.fori_loop(3, 4, two, 0)
    ring_step(4)
    project(lax.rem(z + 4, 8))

    for o in range(1, 4):
        cp = rcopy(csend.at[0], crecv.at[o], cs.at[o], cr.at[o], other)
        cp.wait_recv()
        cp.wait_send()
    summed = csend[y].astype(jnp.float32)
    for o in range(1, 4):
        summed = summed + crecv[o].astype(jnp.float32)
    summed = summed.astype(jnp.bfloat16)
    for n in range(4):
        fsend[n] = summed[:, n * 128 : (n + 1) * 128]
    for n in range(4):
        to_x = (n // 2) * 2 + core
        local = jnp.logical_and(to_x == x, core == n % 2)

        @pl.when(local)
        def _():
            pltpu.make_async_copy(fsend.at[n], frecv.at[x], fr.at[x]).start()

        @pl.when(jnp.logical_not(local))
        def _():
            rcopy(fsend.at[n], frecv.at[x], fs.at[n], fr.at[x], dev(z, to_x, y, n % 2)).start()

    for n in range(4):
        rcopy(fsend.at[n], frecv.at[n], fs.at[n], fr.at[n], other).wait_recv()
    mixed = frecv[...].reshape(896, 128)
    out_ref[...] = jnp.transpose(mixed, (1, 0))

    for n in range(4):
        to_x = (n // 2) * 2 + core

        @pl.when(jnp.logical_not(jnp.logical_and(to_x == x, core == n % 2)))
        def _():
            rcopy(fsend.at[n], frecv.at[n], fs.at[n], fr.at[n], other).wait_send()

    @pl.when(jnp.logical_not(at_home))
    def _():
        rcopy(wt, wbuf.at[wj, xl], w0.at[0], wr.at[wj, xl], other).wait_send()

    @pl.when(core == keeper)
    def _():
        for part in range(2):
            for n in range(2):
                slot = wbuf.at[wj, part]
                rcopy(slot, slot, ws.at[n, wj, part], wr.at[wj, part], other).wait_send()

    for s in range(1, 4):
        for up in (True, False):
            zsrc = lax.rem(z + (8 - s if up else s), 8)
            j = lax.rem(zsrc, 4)

            @pl.when(core == zsrc // 4)
            def _():
                far = 0 if up else 1
                n = 0 if up else 1
                for part, most in ((far, 4), (1 - far, 3)):
                    if s < most:
                        slot = wbuf.at[j, part]
                        rcopy(slot, slot, ws.at[n, j, part], wr.at[j, part], other).wait_send()


def body(queries, latent_rope, key_up, value_up, out_weight, plan):
    flat = plan.reshape(1, 64)
    ids = lax.broadcasted_iota(jnp.int32, (64, 64), 0)
    slots = lax.broadcasted_iota(jnp.int32, (64, 64), 1)
    inv = jnp.sum(jnp.where(flat == ids, slots, 0), axis=1)
    vm = pl.BlockSpec(memory_space=pltpu.VMEM)
    sm = pl.BlockSpec(memory_space=pltpu.SMEM)
    bf, f32 = jnp.bfloat16, jnp.float32
    dma = pltpu.SemaphoreType.DMA
    rows = GROUP * BLOCK
    return pl.pallas_call(
        kernel,
        out_shape=jax.ShapeDtypeStruct((128, 896), bf),
        in_specs=[sm, sm, vm, vm, vm, vm, vm],
        out_specs=vm,
        scratch_shapes=[
            pltpu.VMEM((8, 16, 32, WIDE), bf),
            pltpu.VMEM((2, 2, rows, WIDE), bf),
            pltpu.VMEM((TASKS, rows, 256), f32),
            pltpu.VMEM((TASKS + 1, rows, 128), f32),
            pltpu.VMEM((2, rows, 128), f32),
            pltpu.VMEM((TASKS + 1, rows, 128), f32),
            pltpu.VMEM((TASKS + 1, rows, LATENT), f32),
            pltpu.VMEM((224, 1024), bf),
            pltpu.VMEM((4, 2, 224, 1024), bf),
            pltpu.VMEM((2, 2, 2, 128, 1024), bf),
            pltpu.VMEM((4, 224, 512), bf),
            pltpu.VMEM((4, 224, 512), bf),
            pltpu.VMEM((4, 224, 128), bf),
            pltpu.VMEM((4, 224, 128), bf),
            dma((7,)), dma((7,)), dma((3,)), dma((3,)), dma((4, 2)), dma((4, 2)),
            dma((4, 2)), dma((4, 2)), dma((1,)), dma((2, 4, 2)), dma((4, 2)),
            dma((2, 3)), dma((2, 3)), dma((2, 4)), dma((2, 4)), dma((4,)), dma((4,)),
            dma((4,)), dma((4,)),
        ],
        compiler_params=pltpu.CompilerParams(
            collective_id=0, has_side_effects=True, vmem_limit_bytes=56 * 2**20
        ),
    )(plan, inv, queries, latent_rope, key_up, value_up, out_weight)


def solution(mesh):
    placed = (
        P("ctx", "head"),
        P("ctx", None),
        P(None, "head"),
        P(None, "head"),
        P("head", "ctx"),
        P(),
    )
    return jax.shard_map(
        body, mesh=mesh, in_specs=placed, out_specs=P("ctx", "head"), check_vma=False
    )
```

time: 291 us -> 105 us (0.36); the launches traced: 287 us -> 104 us
  waiting for transfers between devices: 192 us -> 0 us
  Pallas kernels: 0 us -> 97.6 us
  matrix products: 64.7 us -> 0 us
  between operations: 13.2 us -> 0.01 us
  other arithmetic: 11.1 us -> 0.6 us
    all_gather x2 -> x0, waiting for transfers between devices: 155 us -> none  [the longest x1 91.4 us: body(): latent_part = lax.all_gather(latent_rope, 'ctx', axis=0, tiled=True)]
    pallas_call x0 -> x1, Pallas kernels: none -> 97.6 us  [body(): pl.pallas_call(kernel, out_shape=jax.ShapeDtypeStruct((128, 896), bf), in...]
    dot_general x6 -> x0, matrix products: 64.7 us -> none  [the longest x1 13.5 us: attend(): jnp.einsum('hqk,khd->hqd', weights.astype(jnp.bfloat16), value_rows, pref...]
    unnamed x4 -> x0, waiting for transfers between devices: 36.8 us -> none
    reduce_sum x3 -> x1, other arithmetic: 9.22 us -> 0.6 us  [body(): inv = jnp.sum(jnp.where(flat == ids, slots, 0), axis=1)]
    unnamed x10 -> x6, local copies, waits for them, and re-layouts: 6.08 us -> 6.13 us
  transfers between devices with their start and end apart: 3 -> 0, of which waited for: 3 -> 0; matrix products, arithmetic and copies ran while one was open for 24% -> 0% of each run, Pallas kernels for 0% -> 0%
where the time goes in v1:
time: 105 us; the launch traced here: 104 us
  Pallas kernels  97.6 us (93%)
  local copies, waits for them, and re-layouts  6.23 us (6%)
    pallas_call x1, Pallas kernels, body(): pl.pallas_call(kernel, out_shape=jax.ShapeDtypeStruct((128, 896), bf), in...  97.6 us
    unnamed x6, local copies, waits for them, and re-layouts  6.13 us

profile of v1, /device:TPU:1, one launch (start us, length us, event | category | flops | bytes accessed | tf_op | source)
XLA Modules:
  0.0 104.5 jit_solution(1005316346338749592)
XLA Ops:
  0.0 0.8 copy.16.plan_ref
  0.8 0.0 copy-start
  0.8 0.1 eq.10
  0.9 0.6 select_reduce_fusion.inv_ref
  1.5 1.7 %copy.17.lr_ref = bf16[128,576]{1,0:T(8,128)(2,1)} copy(bf16[128,576]{0,1:T(8,128)(2,1)} %param.7) | data formatting | bytes 294912 | tf_op args[1]
  3.2 0.0 copy-done
  3.2 2.0 %copy.18.w_ref = bf16[1024,224]{1,0:T(8,128)(2,1)} copy(bf16[1024,224]{0,1:T(8,128)(2,1)} %param.10) | data formatting | bytes 917504 | tf_op args[4]
  5.2 97.6 %shard_map.64 = bf16[128,896]{1,0:T(8,128)(2,1)} custom-call(s32[32,2]{1,0:T(8,128)} %copy-done, s32[64]{0:T(128)} %select_reduce_fusion.inv_ref, bf16[128,1536]{1,0:T(8,128)(2,1)} %q_ref.1, bf16[128,576]{1,0:T(8,128)(2,1)} %copy.17.lr_ref, bf16[512,1024]{1,0:T(8,128)(2,1)} %ku_ref.1, bf16[512,1024]{1,0:T(8,128)(2,1)} %vu_ref.1, bf16[1024,224]{1,0:T(8,128)(2,1)} %copy.18.w_ref), custom_call_target="tpu_custom_call" | custom-call | tf_op jit(solution)/shard_map/pallas_call | solution.py:408
  102.8 1.6 %copy.20 = bf16[128,896]{1,0:T(8,128)(2,1)} copy(bf16[128,896]{1,0:T(8,128)(2,1)} %shard_map.64) | data formatting | bytes 458752
Async XLA Ops:
  0.8 2.4 %copy-start = (s32[32,2]{1,0:T(8,128)}, s32[32,2]{1,0:T(8,128)S(1)}, u32[]{:S(2)}) copy-start(s32[32,2]{1,0:T(8,128)S(1)} %copy.16.plan_ref) | copy-start | bytes 772

commit v2 on v0

v2 whole, which is shorter than its diff:
```python
import jax
import jax.numpy as jnp
from jax import lax
from jax.experimental import pallas as pl
from jax.experimental.pallas import tpu as pltpu
from jax.sharding import PartitionSpec as P

MESH = pl.DeviceIdType.MESH
NOPE = 128
ROPE = 64
VDIM = 128
LATENT = 512
HEAD_LOCAL = 8
BLOCK = 64
ROWS = HEAD_LOCAL * BLOCK
EARLY = 9
LATE = 8
WIDE = 640
PIECE = 144
NEG = -1e30
SCALE2 = 1.4426950408889634 * (NOPE + ROPE) ** -0.5


def nt(a, b):
    return lax.dot_general(a, b, (((1,), (1,)), ((), ())), preferred_element_type=jnp.float32)


def kernel(
    plan_ref, lrt_ref, q_hbm, ku_hbm, vu_hbm, w_hbm, out_ref,
    place, lat, qv, kuv, vuv, qs, sbuf, mrun, mfin, lrun, acc, wbuf, att, csend, crecv,
    ls, zs, zr, xs, xr, ys, yr, ks, kr, w0, ws, wr, as_, ar, bs, br, cs, cr,
):
    ctx = lax.axis_index("ctx")
    head = lax.axis_index("head")
    core = lax.rem(ctx, 2)
    xh = lax.rem(ctx // 2, 2)
    z = ctx // 4
    xl = head // 4
    y = lax.rem(head, 4)
    x = xh * 2 + xl

    def dev(z_, x_, y_, c_):
        return ((z_ * 2 + x_ // 2) * 2 + c_, lax.rem(x_, 2) * 4 + y_)

    def zdev(d):
        return dev(lax.rem(z + d, 8), x, y, core)

    def xdev(o):
        return dev(z, lax.rem(x + o, 4), y, core)

    def ydev(o):
        return dev(z, x, lax.rem(y + o, 4), core)

    other = dev(z, x, y, 1 - core)

    def rcopy(src, dst, ssem, rsem, target):
        return pltpu.make_async_remote_copy(
            src_ref=src, dst_ref=dst, send_sem=ssem, recv_sem=rsem,
            device_id=target, device_id_type=MESH,
        )

    barrier = pltpu.get_barrier_semaphore()
    for d in range(1, 8):
        pl.semaphore_signal(barrier, 1, device_id=zdev(d), device_id_type=MESH)
    for oy in range(4):
        for ox in range(4):
            for oc in range(2):
                if oy or ox or oc:
                    pl.semaphore_signal(
                        barrier, 1,
                        device_id=dev(z, lax.rem(x + ox, 4), lax.rem(y + oy, 4), lax.rem(core + oc, 2)),
                        device_id_type=MESH,
                    )
    loads = [
        pltpu.make_async_copy(q_hbm, qv, ls.at[0]),
        pltpu.make_async_copy(ku_hbm, kuv, ls.at[1]),
        pltpu.make_async_copy(vu_hbm, vuv, ls.at[2]),
    ]
    for cp in loads:
        cp.start()

    def place_of(b, carry):
        found = jnp.int32(0)
        for c in range(32):
            found = jnp.where(jnp.minimum(plan_ref[0, c], plan_ref[1, c]) == b, c, found)
        place[b] = found
        return carry

    lax.fori_loop(0, 32, place_of, 0)

    par = lax.rem(y, 2)

    def piece(src_x, parity, c_):
        return (src_x // 2) * 8 + c_ * 4 + parity * 2 + lax.rem(src_x, 2)

    mine = piece(x, par, core)
    rows_all = jnp.transpose(lrt_ref[...], (1, 0))
    quarter = par * 2 + xl
    for q in range(4):
        @pl.when(quarter == q)
        def _():
            part = rows_all[q * 32 : (q + 1) * 32]
            for c in range(4):
                lat[z, mine, c * 32 : (c + 1) * 32] = part[:, c * 128 : (c + 1) * 128]
            rope = part[:, LATENT:]
            lat[z, mine, 128:PIECE] = jnp.concatenate([rope[:16], rope[16:]], axis=1)

    def dist(i):
        if isinstance(i, int):
            return 0
        return lax.rem(jnp.where(lax.rem(i, 2) == 1, (i + 1) // 2, 8 - i // 2), 8)

    def source(i):
        return lax.rem(z + 8 - dist(i), 8)

    def spread(o, i, zsrc, idx):
        slot = lat.at[zsrc, idx]
        to = lax.rem(y + 1 + 2 * (i % 2), 4)
        rcopy(slot, slot, ys.at[o, i], yr.at[o, i], dev(z, x, to, core)).start()
        rcopy(slot, slot, ks.at[o, i], kr.at[o, i], other).start()

    pair = x + 1 - 2 * xl
    cross = 3 - x
    origin = (x, pair, cross, lax.rem(x + 2, 4))

    def from_z(i):
        zsrc = source(i)
        slot = lat.at[zsrc, mine]
        d = dist(i)

        if not isinstance(i, int):
            rcopy(slot, slot, zs.at[d], zr.at[d], other).wait_recv()
        rcopy(slot, slot, xs.at[1, i], xr.at[1, i], dev(z, pair, y, core)).start()
        rcopy(slot, slot, xs.at[2, i], xr.at[2, i], dev(z, cross, y, core)).start()
        spread(0, i, zsrc, mine)

    def from_x(i, o):
        zsrc = source(i)
        idx = piece(origin[o], par, core)
        slot = lat.at[zsrc, idx]
        rcopy(slot, slot, xs.at[o, i], xr.at[o, i], other).wait_recv()
        if o == 1:
            rcopy(slot, slot, xs.at[3, i], xr.at[3, i], dev(z, cross, y, core)).start()
        spread(o, i, zsrc, idx)

    def from_y(i):
        zsrc = source(i)
        for o in range(4):
            idx = piece(origin[o], 1 - par, core)
            slot = lat.at[zsrc, idx]
            rcopy(slot, slot, ys.at[o, i], yr.at[o, i], other).wait_recv()
            rcopy(slot, slot, ks.at[4 + o, i], kr.at[4 + o, i], other).start()

    def stage(m, carry):
        @pl.when(m < 4)
        def _():
            from_z(2 * m + 1)

        @pl.when(m < 3)
        def _():
            from_z(2 * m + 2)

        @pl.when(m < 8)
        def _():
            from_x(m, 1)
            from_x(m, 2)

        @pl.when(jnp.logical_and(m >= 1, m < 9))
        def _():
            from_x(m - 1, 3)

        @pl.when(m >= 3)
        def _():
            from_y(m - 3)

        return carry

    pl.semaphore_wait(barrier, 38)

    for d in (1, 7, 2, 6, 3, 5, 4):
        rcopy(lat.at[z, mine], lat.at[z, mine], zs.at[d], zr.at[d], zdev(d)).start()

    from_z(0)

    wj = lax.rem(z, 4)
    keeper = z // 4
    at_home = jnp.logical_and(core == xl, core == keeper)

    @pl.when(at_home)
    def _():
        pltpu.make_async_copy(w_hbm, wbuf.at[wj, xl], wr.at[wj, xl]).start()

    @pl.when(jnp.logical_not(at_home))
    def _():
        rcopy(
            w_hbm, wbuf.at[wj, xl], w0.at[0], wr.at[wj, xl], dev(z, xh * 2 + core, y, keeper)
        ).start()

    for cp in loads:
        cp.wait()
    for h in range(HEAD_LOCAL):
        lo = h * (NOPE + ROPE)
        qn = qv[:, lo : lo + NOPE]
        qr = qv[:, lo + NOPE : lo + NOPE + ROPE].astype(jnp.float32) * SCALE2
        qr = qr.astype(jnp.bfloat16)
        ql = (nt(qn, kuv[:, h * NOPE : (h + 1) * NOPE]) * SCALE2).astype(jnp.bfloat16)
        qr = jnp.concatenate([qr, qr], axis=1)
        for i in range(2):
            qs[i, h * BLOCK : (h + 1) * BLOCK, 0:LATENT] = ql[i * BLOCK : (i + 1) * BLOCK]
            qs[i, h * BLOCK : (h + 1) * BLOCK, LATENT:WIDE] = qr[i * BLOCK : (i + 1) * BLOCK]

    def ring_send(j, part, up):
        slot = wbuf.at[j, part]
        n = 0 if up else 1
        rcopy(slot, slot, ws.at[n, j, part], wr.at[j, part], zdev(1 if up else 7)).start()

    def ring_wait(j, part):
        slot = wbuf.at[j, part]
        rcopy(slot, slot, w0.at[0], wr.at[j, part], other).wait_recv()

    def ring_step(s):
        if s == 0:
            @pl.when(core == keeper)
            def _():
                for part in range(2):
                    ring_wait(wj, part)
                for part in range(2):
                    ring_send(wj, part, True)
                    ring_send(wj, part, False)
            return
        for up in (True, False):
            zsrc = lax.rem(z + (8 - s if up else s), 8)
            j = lax.rem(zsrc, 4)

            @pl.when(core == zsrc // 4)
            def _():
                far = 0 if up else 1
                if s <= 4:
                    ring_wait(j, far)
                if s <= 3:
                    ring_wait(j, 1 - far)
                if s < 4:
                    ring_send(j, far, up)
                if s < 3:
                    ring_send(j, 1 - far, up)

    lax.fori_loop(0, 2, stage, 0)
    ring_step(0)
    lax.fori_loop(2, 8, stage, 0)
    ring_step(1)
    lax.fori_loop(8, 11, stage, 0)

    def core_wait(i, carry):
        zsrc = source(i)
        for o in range(4):
            for n, parity in ((0, par), (4, 1 - par)):
                slot = lat.at[zsrc, piece(origin[o], parity, 1 - core)]
                rcopy(slot, slot, ks.at[n + o, i], kr.at[n + o, i], other).wait_recv()
        return carry

    lax.fori_loop(0, 8, core_wait, 0)

    p0 = plan_ref[0, ctx]
    p1 = plan_ref[1, ctx]
    low = jnp.minimum(p0, p1)
    high = jnp.maximum(p0, p1)
    low_at = jnp.where(p0 < p1, 0, 1)
    beta = lax.div(low, 4)
    row_of = lax.broadcasted_iota(jnp.int32, (ROWS, 256), 0) % BLOCK
    ahead = lax.broadcasted_iota(jnp.int32, (ROWS, 256), 1) - row_of
    left = lax.broadcasted_iota(jnp.int32, (16, 128), 1) < 64
    none = jnp.zeros((16, 128), jnp.bfloat16)

    def chunk_of(t):
        return jnp.where(t <= beta, t, t - beta - 1)

    def pieces_of(t):
        first = chunk_of(t) * 4
        got = []
        for i in range(4):
            c = place[jnp.minimum(first + i, 63 - first - i)]
            s = 2 * c + jnp.where(plan_ref[0, c] == first + i, 0, 1)
            pair = lat[lax.div(s, 8), pl.ds(lax.rem(s, 8) * 2, 2)]
            got += [pair[0], pair[1]]
        return got

    def wide_of(got):
        return jnp.concatenate(
            [
                jnp.concatenate([p[c * 32 : (c + 1) * 32] for p in got], axis=0)
                for c in range(4)
            ],
            axis=1,
        )

    def keys_of(t):
        got = pieces_of(t)
        rope = []
        for p in got:
            r = p[128:PIECE]
            rope += [jnp.where(left, r, none), jnp.where(left, none, r)]
        return jnp.concatenate([wide_of(got), jnp.concatenate(rope, axis=0)], axis=1)

    def values_of(t):
        return wide_of(pieces_of(t))

    def fold(s):
        return jnp.maximum(s[:, :128], s[:, 128:])

    mrun[0] = jnp.full((ROWS, 128), NEG, jnp.float32)
    lrun[0] = jnp.zeros((ROWS, 128), jnp.float32)
    acc[0] = jnp.zeros((ROWS, LATENT), jnp.float32)

    def score(t, carry):
        is_low = t <= beta
        q = qs[jnp.where(is_low, low_at, 1 - low_at)]
        s = nt(q, keys_of(t))
        room = jnp.where(is_low, low, high) * BLOCK - chunk_of(t) * 256
        s = jnp.where(ahead <= room, s, NEG)
        sbuf[t] = s
        before = jnp.where(t == beta + 1, NEG, mrun[t])
        mrun[t + 1] = jnp.maximum(before, fold(s))
        return carry

    def row_max(at):
        return jnp.broadcast_to(jnp.max(mrun[at], axis=1, keepdims=True), (ROWS, 128))

    def weights(s, m):
        wa = jnp.exp2(s[:, :128] - m)
        wb = jnp.exp2(s[:, 128:] - m)
        return wa + wb, jnp.concatenate([wa, wb], axis=1).astype(jnp.bfloat16)

    def weigh(t, carry):
        is_low = t <= beta
        keep = jnp.where(t == beta + 1, 0.0, 1.0)
        total, w = weights(sbuf[t], mfin[jnp.where(is_low, 0, 1)])
        lrun[t + 1] = lrun[t] * keep + total
        added = jnp.dot(w, values_of(t), preferred_element_type=jnp.float32)
        acc[t + 1] = acc[t] * keep + added
        return carry

    def normal(at):
        total = jnp.sum(lrun[at], axis=1, keepdims=True)
        return (acc[at] / total).astype(jnp.bfloat16)

    def shard(half, src_x, c_):
        return att.at[half, lax.rem(src_x, 2), src_x // 2, c_]

    def finish(half, o):
        for h in range(HEAD_LOCAL):
            up = jnp.dot(
                o[h * BLOCK : (h + 1) * BLOCK],
                vuv[:, h * VDIM : (h + 1) * VDIM],
                preferred_element_type=jnp.float32,
            )
            att[half, xl, xh, core, :, h * VDIM : (h + 1) * VDIM] = up.astype(jnp.bfloat16)
        here = shard(half, x, core)
        for n in (1, 3, 2):
            rcopy(here, here, as_.at[half, n], ar.at[half, n], xdev(n)).start()
        rcopy(here, here, bs.at[half, 0], br.at[half, 0], other).start()

    def pass_on(half):
        for n in (1, 3, 2):
            there = shard(half, lax.rem(x + 4 - n, 4), core)
            rcopy(there, there, as_.at[half, n], ar.at[half, n], other).wait_recv()
            rcopy(there, there, bs.at[half, n], br.at[half, n], other).start()

    def gathered(half):
        for n in range(4):
            there = shard(half, lax.rem(x + 4 - n, 4), 1 - core)
            rcopy(there, there, bs.at[half, n], br.at[half, n], other).wait_recv()

    lax.fori_loop(0, EARLY, score, 0)
    mfin[0] = row_max(beta + 1)
    mfin[1] = row_max(EARLY)
    ring_step(2)
    lax.fori_loop(0, EARLY, weigh, 0)
    finish(0, normal(beta + 1))

    def late_score(i, carry):
        t = EARLY + i
        s = nt(qs[1 - low_at], keys_of(t))
        room = high * BLOCK - chunk_of(t) * 256
        s = jnp.where(ahead <= room, s, NEG)
        sbuf[i] = s
        mrun[t + 1] = jnp.maximum(mrun[t], fold(s))
        return carry

    lax.fori_loop(0, LATE, late_score, 0)
    mfin[0] = row_max(EARLY + LATE)
    again = jnp.exp2(mfin[1] - mfin[0])
    lrun[EARLY] = lrun[EARLY] * again
    acc[EARLY] = acc[EARLY] * jnp.concatenate([again] * 4, axis=1)
    pass_on(0)

    def late_weigh(i, carry):
        m = mfin[0]
        total, w = weights(sbuf[2 * i], m)
        total2, w2 = weights(sbuf[2 * i + 1], m)
        lrun[EARLY] = lrun[EARLY] + (total + total2)
        v = jnp.concatenate([values_of(EARLY + 2 * i), values_of(EARLY + 2 * i + 1)], axis=0)
        acc[EARLY] = acc[EARLY] + jnp.dot(
            jnp.concatenate([w, w2], axis=1), v, preferred_element_type=jnp.float32
        )
        return carry

    lax.fori_loop(0, LATE // 2, late_weigh, 0)
    finish(1, normal(EARLY))

    def project(half, zsrc):
        j = lax.rem(zsrc, 4)

        @pl.when(core == zsrc // 4)
        def _():
            total = nt(wbuf[j, 0], att[half, 0].reshape(256, 1024)) + nt(
                wbuf[j, 1], att[half, 1].reshape(256, 1024)
            )
            total = total.astype(jnp.bfloat16)
            for n in range(4):
                lanes = total[:, n * BLOCK : (n + 1) * BLOCK]
                csend[half, j, n] = jnp.concatenate([lanes[:112], lanes[112:]], axis=1)
            for n in range(4):
                to_x = (n // 2) * 2 + core
                local = jnp.logical_and(jnp.logical_and(to_x == x, core == n % 2), j == y)

                @pl.when(local)
                def _():
                    pltpu.make_async_copy(
                        csend.at[half, j, n], crecv.at[half, y, x], cr.at[half, y, x]
                    ).start()

                @pl.when(jnp.logical_not(local))
                def _():
                    rcopy(
                        csend.at[half, j, n], crecv.at[half, y, x], cs.at[half, j, n],
                        cr.at[half, y, x], dev(z, to_x, j, n % 2),
                    ).start()

    def both(half, s):
        project(half, lax.rem(z + 8 - s, 8))
        project(half, lax.rem(z + s, 8))

    def near(half):
        def loop(s, carry):
            both(half, s)
            return carry

        project(half, z)
        lax.fori_loop(1, 3, loop, 0)

    ring_step(3)
    gathered(0)
    near(0)
    both(0, 3)
    ring_step(4)
    project(0, lax.rem(z + 4, 8))
    pass_on(1)
    gathered(1)
    near(1)
    both(1, 3)
    project(1, lax.rem(z + 4, 8))

    halves = []
    for half in range(2):
        columns = []
        for n in range(4):
            total = None
            for m in range(4):
                slot = crecv.at[half, m, n]
                rcopy(slot, slot, cs.at[half, m, n], cr.at[half, m, n], other).wait_recv()
                term = slot[...].astype(jnp.float32)
                total = term if total is None else total + term
            columns += [total[:, :BLOCK], total[:, BLOCK:]]
        halves.append(jnp.concatenate(columns, axis=0))
    first = jnp.where(low_at == 0, halves[0], halves[1])
    second = jnp.where(low_at == 0, halves[1], halves[0])
    mixed = jnp.concatenate([first, second], axis=1)
    out_ref[...] = jnp.transpose(mixed, (1, 0)).astype(jnp.bfloat16)

    for d in range(1, 8):
        slot = lat.at[z, mine]
        rcopy(slot, slot, zs.at[d], zr.at[d], other).wait_send()

    def left_core(i, carry):
        slot = lat.at[z, mine]
        for o in range(4):
            if o:
                rcopy(slot, slot, xs.at[o, i], xr.at[o, i], other).wait_send()
            rcopy(slot, slot, ys.at[o, i], yr.at[o, i], other).wait_send()
            rcopy(slot, slot, ks.at[o, i], kr.at[o, i], other).wait_send()
            rcopy(slot, slot, ks.at[4 + o, i], kr.at[4 + o, i], other).wait_send()
        return carry

    lax.fori_loop(0, 8, left_core, 0)
    for half in range(2):
        here = shard(half, x, core)
        for n in range(4):
            if n:
                rcopy(here, here, as_.at[half, n], ar.at[half, n], other).wait_send()
            rcopy(here, here, bs.at[half, n], br.at[half, n], other).wait_send()
        for j in range(4):
            for n in range(4):
                to_x = (n // 2) * 2 + core
                local = jnp.logical_and(jnp.logical_and(to_x == x, core == n % 2), j == y)

                @pl.when(jnp.logical_not(local))
                def _():
                    slot = csend.at[half, j, n]
                    rcopy(slot, slot, cs.at[half, j, n], cr.at[half, j, n], other).wait_send()

    @pl.when(jnp.logical_not(at_home))
    def _():
        rcopy(w_hbm, wbuf.at[wj, xl], w0.at[0], wr.at[wj, xl], other).wait_send()

    @pl.when(core == keeper)
    def _():
        for part in range(2):
            for n in range(2):
                slot = wbuf.at[wj, part]
                rcopy(slot, slot, ws.at[n, wj, part], wr.at[wj, part], other).wait_send()

    for s in range(1, 4):
        for up in (True, False):
            zsrc = lax.rem(z + (8 - s if up else s), 8)
            j = lax.rem(zsrc, 4)

            @pl.when(core == zsrc // 4)
            def _():
                far = 0 if up else 1
                n = 0 if up else 1
                for part, most in ((far, 4), (1 - far, 3)):
                    if s < most:
                        slot = wbuf.at[j, part]
                        rcopy(slot, slot, ws.at[n, j, part], wr.at[j, part], other).wait_send()


def body(queries, latent_rope, key_up, value_up, out_weight, plan):
    vm = pl.BlockSpec(memory_space=pltpu.VMEM)
    sm = pl.BlockSpec(memory_space=pltpu.SMEM)
    anywhere = pl.BlockSpec(memory_space=pl.ANY)
    bf, f32 = jnp.bfloat16, jnp.float32
    dma = pltpu.SemaphoreType.DMA
    return pl.pallas_call(
        kernel,
        out_shape=jax.ShapeDtypeStruct((128, 896), bf),
        in_specs=[sm, vm, anywhere, anywhere, anywhere, anywhere],
        out_specs=vm,
        scratch_shapes=[
            pltpu.SMEM((32,), jnp.int32),
            pltpu.VMEM((8, 16, PIECE, 128), bf),
            pltpu.VMEM((128, 1536), bf),
            pltpu.VMEM((512, 1024), bf),
            pltpu.VMEM((512, 1024), bf),
            pltpu.VMEM((2, ROWS, WIDE), bf),
            pltpu.VMEM((EARLY, ROWS, 256), f32),
            pltpu.VMEM((EARLY + LATE + 1, ROWS, 128), f32),
            pltpu.VMEM((2, ROWS, 128), f32),
            pltpu.VMEM((EARLY + 1, ROWS, 128), f32),
            pltpu.VMEM((EARLY + 1, ROWS, LATENT), f32),
            pltpu.VMEM((4, 2, 224, 1024), bf),
            pltpu.VMEM((2, 2, 2, 2, BLOCK, 1024), bf),
            pltpu.VMEM((2, 4, 4, 112, 128), bf),
            pltpu.VMEM((2, 4, 4, 112, 128), bf),
            dma((3,)), dma((8,)), dma((8,)), dma((4, 8)), dma((4, 8)), dma((4, 8)), dma((4, 8)),
            dma((8, 8)), dma((8, 8)), dma((1,)), dma((2, 4, 2)), dma((4, 2)),
            dma((2, 4)), dma((2, 4)), dma((2, 4)), dma((2, 4)), dma((2, 4, 4)), dma((2, 4, 4)),
        ],
        compiler_params=pltpu.CompilerParams(
            collective_id=0, has_side_effects=True, vmem_limit_bytes=56 * 2**20
        ),
    )(plan.T, latent_rope.T, queries, key_up, value_up, out_weight.T)


def solution(mesh):
    placed = (
        P("ctx", "head"),
        P("ctx", None),
        P(None, "head"),
        P(None, "head"),
        P("head", "ctx"),
        P(),
    )
    return jax.shard_map(
        body, mesh=mesh, in_specs=placed, out_specs=P("ctx", "head"), check_vma=False
    )
```

time: 291 us -> 84 us (0.29)
  the two profiles are of different devices: /device:TPU:1 before, /device:TPU:7 now
where the time goes in v2:
time: 84 us; the launch traced here: 83.9 us
  Pallas kernels  82.2 us (98%)
  local copies, waits for them, and re-layouts  1.65 us (2%)
    pallas_call x1, Pallas kernels, body(): pl.pallas_call(kernel, out_shape=jax.ShapeDtypeStruct((128, 896), bf), in...  82.2 us

profile of v2, /device:TPU:7, one launch (start us, length us, event | category | flops | bytes accessed | tf_op | source)
XLA Modules:
  0.0 83.9 jit_solution(8042079344158509790)
XLA Ops:
  0.0 82.2 %shard_map.64 = bf16[128,896]{1,0:T(8,128)(2,1)} custom-call(s32[2,32]{1,0:T(2,128)} %bitcast.5, bf16[576,128]{1,0:T(8,128)(2,1)} %bitcast.4, bf16[128,1536]{1,0:T(8,128)(2,1)} %q_hbm.1, bf16[512,1024]{1,0:T(8,128)(2,1)} %ku_hbm.1, bf16[512,1024]{1,0:T(8,128)(2,1)} %vu_hbm.1, bf16[224,1024]{1,0:T(8,128)(2,1)} %bitcast.3), custom_call_target="tpu_custom_call" | custom-call | tf_op jit(solution)/shard_map/pallas_call | solution.py:543
  82.2 1.6 %copy.8 = bf16[128,896]{1,0:T(8,128)(2,1)} copy(bf16[128,896]{1,0:T(8,128)(2,1)} %shard_map.64) | data formatting | bytes 458752

commit v3 on v2

v3 whole, which is shorter than its diff:
```python
import jax
import jax.numpy as jnp
from jax import lax
from jax.experimental import pallas as pl
from jax.experimental.pallas import tpu as pltpu
from jax.sharding import PartitionSpec as P

MESH = pl.DeviceIdType.MESH
NOPE = 128
ROPE = 64
VDIM = 128
LATENT = 512
HEAD_LOCAL = 8
BLOCK = 64
ROWS = HEAD_LOCAL * BLOCK
EARLY = 9
LATE = 8
WIDE = 640
PIECE = 144
NEG = -1e30
SCALE2 = 1.4426950408889634 * (NOPE + ROPE) ** -0.5


def nt(a, b):
    return lax.dot_general(a, b, (((1,), (1,)), ((), ())), preferred_element_type=jnp.float32)


def kernel(
    plan_ref, lrt_hbm, q_hbm, ku_hbm, vu_hbm, w_hbm, out_ref,
    place, lrt, lat, qv, kuv, vuv, qs, sbuf, mrun, mfin, lrun, acc, wbuf, att, csend, crecv,
    ls, zs, zr, xs, xr, ys, yr, ks, kr, w0, ws, wr, as_, ar, bs, br, cs, cr,
):
    ctx = lax.axis_index("ctx")
    head = lax.axis_index("head")
    core = lax.rem(ctx, 2)
    xh = lax.rem(ctx // 2, 2)
    z = ctx // 4
    xl = head // 4
    y = lax.rem(head, 4)
    x = xh * 2 + xl

    def dev(z_, x_, y_, c_):
        return ((z_ * 2 + x_ // 2) * 2 + c_, lax.rem(x_, 2) * 4 + y_)

    def zdev(d):
        return dev(lax.rem(z + d, 8), x, y, core)

    def xdev(o):
        return dev(z, lax.rem(x + o, 4), y, core)

    def ydev(o):
        return dev(z, x, lax.rem(y + o, 4), core)

    other = dev(z, x, y, 1 - core)

    def rcopy(src, dst, ssem, rsem, target):
        return pltpu.make_async_remote_copy(
            src_ref=src, dst_ref=dst, send_sem=ssem, recv_sem=rsem,
            device_id=target, device_id_type=MESH,
        )

    loads = [
        pltpu.make_async_copy(lrt_hbm, lrt, ls.at[3]),
        pltpu.make_async_copy(q_hbm, qv, ls.at[0]),
        pltpu.make_async_copy(ku_hbm, kuv, ls.at[1]),
        pltpu.make_async_copy(vu_hbm, vuv, ls.at[2]),
    ]
    for cp in loads:
        cp.start()

    barrier = pltpu.get_barrier_semaphore()
    for d in range(1, 8):
        pl.semaphore_signal(barrier, 1, device_id=zdev(d), device_id_type=MESH)
    for oy in range(4):
        for ox in range(4):
            for oc in range(2):
                if oy or ox or oc:
                    pl.semaphore_signal(
                        barrier, 1,
                        device_id=dev(z, lax.rem(x + ox, 4), lax.rem(y + oy, 4), lax.rem(core + oc, 2)),
                        device_id_type=MESH,
                    )
    par = lax.rem(y, 2)

    def piece(src_x, parity, c_):
        return (src_x // 2) * 8 + c_ * 4 + parity * 2 + lax.rem(src_x, 2)

    mine = piece(x, par, core)
    loads[0].wait()
    rows_all = jnp.transpose(lrt[...], (1, 0))
    quarter = par * 2 + xl
    for q in range(4):
        @pl.when(quarter == q)
        def _():
            part = rows_all[q * 32 : (q + 1) * 32]
            for c in range(4):
                lat[z, mine, c * 32 : (c + 1) * 32] = part[:, c * 128 : (c + 1) * 128]
            rope = part[:, LATENT:]
            lat[z, mine, 128:PIECE] = jnp.concatenate([rope[:16], rope[16:]], axis=1)

    def dist(i):
        if isinstance(i, int):
            return 0
        return lax.rem(jnp.where(lax.rem(i, 2) == 1, (i + 1) // 2, 8 - i // 2), 8)

    def source(i):
        return lax.rem(z + 8 - dist(i), 8)

    def spread(o, i, zsrc, idx):
        slot = lat.at[zsrc, idx]
        to = lax.rem(y + 1 + 2 * (i % 2), 4)
        rcopy(slot, slot, ys.at[0], yr.at[o, i], dev(z, x, to, core)).start()
        rcopy(slot, slot, ks.at[0], kr.at[0], other).start()

    pair = x + 1 - 2 * xl
    cross = 3 - x
    origin = (x, pair, cross, lax.rem(x + 2, 4))

    def from_z(i):
        zsrc = source(i)
        slot = lat.at[zsrc, mine]
        d = dist(i)

        if not isinstance(i, int):
            rcopy(slot, slot, zs.at[0], zr.at[d], other).wait_recv()
        rcopy(slot, slot, xs.at[0], xr.at[1, i], dev(z, pair, y, core)).start()
        rcopy(slot, slot, xs.at[0], xr.at[2, i], dev(z, cross, y, core)).start()
        spread(0, i, zsrc, mine)

    def from_x(i, o):
        zsrc = source(i)
        idx = piece(origin[o], par, core)
        slot = lat.at[zsrc, idx]
        rcopy(slot, slot, xs.at[0], xr.at[o, i], other).wait_recv()
        if o == 1:
            rcopy(slot, slot, xs.at[0], xr.at[3, i], dev(z, cross, y, core)).start()
        spread(o, i, zsrc, idx)

    def from_y(i):
        zsrc = source(i)
        for o in range(4):
            idx = piece(origin[o], 1 - par, core)
            slot = lat.at[zsrc, idx]
            rcopy(slot, slot, ys.at[0], yr.at[o, i], other).wait_recv()
            rcopy(slot, slot, ks.at[0], kr.at[0], other).start()

    def stage(m, carry):
        @pl.when(m < 4)
        def _():
            from_z(2 * m + 1)

        @pl.when(m < 3)
        def _():
            from_z(2 * m + 2)

        @pl.when(m < 8)
        def _():
            from_x(m, 1)
            from_x(m, 2)

        @pl.when(jnp.logical_and(m >= 1, m < 9))
        def _():
            from_x(m - 1, 3)

        @pl.when(m >= 3)
        def _():
            from_y(m - 3)

        return carry

    pl.semaphore_wait(barrier, 38)

    for d in (1, 7, 2, 6, 3, 5, 4):
        rcopy(lat.at[z, mine], lat.at[z, mine], zs.at[0], zr.at[d], zdev(d)).start()

    from_z(0)

    wj = lax.rem(z, 4)
    keeper = z // 4
    at_home = jnp.logical_and(core == xl, core == keeper)

    @pl.when(at_home)
    def _():
        pltpu.make_async_copy(w_hbm, wbuf.at[wj, xl], wr.at[wj, xl]).start()

    @pl.when(jnp.logical_not(at_home))
    def _():
        rcopy(
            w_hbm, wbuf.at[wj, xl], w0.at[0], wr.at[wj, xl], dev(z, xh * 2 + core, y, keeper)
        ).start()

    def place_of(b, carry):
        found = jnp.int32(0)
        for c in range(32):
            found = jnp.where(jnp.minimum(plan_ref[0, c], plan_ref[1, c]) == b, c, found)
        place[b] = found
        return carry

    lax.fori_loop(0, 32, place_of, 0)

    for cp in loads[1:]:
        cp.wait()
    for h in range(HEAD_LOCAL):
        lo = h * (NOPE + ROPE)
        qn = qv[:, lo : lo + NOPE]
        qr = qv[:, lo + NOPE : lo + NOPE + ROPE].astype(jnp.float32) * SCALE2
        qr = qr.astype(jnp.bfloat16)
        ql = (nt(qn, kuv[:, h * NOPE : (h + 1) * NOPE]) * SCALE2).astype(jnp.bfloat16)
        qr = jnp.concatenate([qr, qr], axis=1)
        for i in range(2):
            qs[i, h * BLOCK : (h + 1) * BLOCK, 0:LATENT] = ql[i * BLOCK : (i + 1) * BLOCK]
            qs[i, h * BLOCK : (h + 1) * BLOCK, LATENT:WIDE] = qr[i * BLOCK : (i + 1) * BLOCK]

    def ring_send(j, part, up):
        slot = wbuf.at[j, part]
        n = 0 if up else 1
        rcopy(slot, slot, ws.at[n, j, part], wr.at[j, part], zdev(1 if up else 7)).start()

    def ring_wait(j, part):
        slot = wbuf.at[j, part]
        rcopy(slot, slot, w0.at[0], wr.at[j, part], other).wait_recv()

    def ring_moves(s, q):
        part = xl if q == 0 else 1 - xl
        for up in (True, False):
            reach = jnp.where((part == 0) == up, 4, 3)
            yield up, part, lax.rem(z + (8 - s if up else s), 8), reach

    def ring_step(s, q):
        if s == 0:
            part = xl if q == 0 else 1 - xl

            @pl.when(core == keeper)
            def _():
                ring_wait(wj, part)
                ring_send(wj, part, True)
                ring_send(wj, part, False)
            return
        for up, part, zsrc, reach in ring_moves(s, q):
            j = lax.rem(zsrc, 4)

            @pl.when(jnp.logical_and(core == zsrc // 4, s <= reach))
            def _():
                ring_wait(j, part)

            @pl.when(jnp.logical_and(core == zsrc // 4, s < reach))
            def _():
                ring_send(j, part, up)

    ring_step(0, 0)
    lax.fori_loop(0, 2, stage, 0)
    ring_step(0, 1)
    lax.fori_loop(2, 3, stage, 0)
    ring_step(1, 0)
    lax.fori_loop(3, 6, stage, 0)
    ring_step(1, 1)
    lax.fori_loop(6, 9, stage, 0)
    ring_step(2, 0)
    lax.fori_loop(9, 11, stage, 0)

    many = lat.at[pl.ds(0, 4)]
    rcopy(many, many, ks.at[0], kr.at[0], other).wait_recv()
    ring_step(2, 1)

    p0 = plan_ref[0, ctx]
    p1 = plan_ref[1, ctx]
    low = jnp.minimum(p0, p1)
    high = jnp.maximum(p0, p1)
    low_at = jnp.where(p0 < p1, 0, 1)
    beta = lax.div(low, 4)
    row_of = lax.broadcasted_iota(jnp.int32, (ROWS, 256), 0) % BLOCK
    ahead = lax.broadcasted_iota(jnp.int32, (ROWS, 256), 1) - row_of
    left = lax.broadcasted_iota(jnp.int32, (16, 128), 1) < 64
    none = jnp.zeros((16, 128), jnp.bfloat16)

    def chunk_of(t):
        return jnp.where(t <= beta, t, t - beta - 1)

    def pieces_of(t):
        first = chunk_of(t) * 4
        got = []
        for i in range(4):
            c = place[jnp.minimum(first + i, 63 - first - i)]
            s = 2 * c + jnp.where(plan_ref[0, c] == first + i, 0, 1)
            pair = lat[lax.div(s, 8), pl.ds(lax.rem(s, 8) * 2, 2)]
            got += [pair[0], pair[1]]
        return got

    def wide_of(got):
        return jnp.concatenate(
            [
                jnp.concatenate([p[c * 32 : (c + 1) * 32] for p in got], axis=0)
                for c in range(4)
            ],
            axis=1,
        )

    def keys_of(t):
        got = pieces_of(t)
        rope = []
        for p in got:
            r = p[128:PIECE]
            rope += [jnp.where(left, r, none), jnp.where(left, none, r)]
        return jnp.concatenate([wide_of(got), jnp.concatenate(rope, axis=0)], axis=1)

    def values_of(t):
        return wide_of(pieces_of(t))

    def fold(s):
        return jnp.maximum(s[:, :128], s[:, 128:])

    mrun[0] = jnp.full((ROWS, 128), NEG, jnp.float32)
    lrun[0] = jnp.zeros((ROWS, 128), jnp.float32)
    acc[0] = jnp.zeros((ROWS, LATENT), jnp.float32)

    def score(t, carry):
        is_low = t <= beta
        q = qs[jnp.where(is_low, low_at, 1 - low_at)]
        s = nt(q, keys_of(t))
        room = jnp.where(is_low, low, high) * BLOCK - chunk_of(t) * 256
        s = jnp.where(ahead <= room, s, NEG)
        sbuf[t] = s
        before = jnp.where(t == beta + 1, NEG, mrun[t])
        mrun[t + 1] = jnp.maximum(before, fold(s))
        return carry

    def row_max(at):
        return jnp.broadcast_to(jnp.max(mrun[at], axis=1, keepdims=True), (ROWS, 128))

    def weights(s, m):
        wa = jnp.exp2(s[:, :128] - m)
        wb = jnp.exp2(s[:, 128:] - m)
        return wa + wb, jnp.concatenate([wa, wb], axis=1).astype(jnp.bfloat16)

    def weigh(t, carry):
        is_low = t <= beta
        keep = jnp.where(t == beta + 1, 0.0, 1.0)
        total, w = weights(sbuf[t], mfin[jnp.where(is_low, 0, 1)])
        lrun[t + 1] = lrun[t] * keep + total
        added = jnp.dot(w, values_of(t), preferred_element_type=jnp.float32)
        acc[t + 1] = acc[t] * keep + added
        return carry

    def normal(at):
        total = jnp.sum(lrun[at], axis=1, keepdims=True)
        return (acc[at] / total).astype(jnp.bfloat16)

    def shard(half, src_x, c_):
        return att.at[half, lax.rem(src_x, 2), src_x // 2, c_]

    def finish(half, o):
        for h in range(HEAD_LOCAL):
            up = jnp.dot(
                o[h * BLOCK : (h + 1) * BLOCK],
                vuv[:, h * VDIM : (h + 1) * VDIM],
                preferred_element_type=jnp.float32,
            )
            att[half, xl, xh, core, :, h * VDIM : (h + 1) * VDIM] = up.astype(jnp.bfloat16)
        here = shard(half, x, core)
        for n in (1, 3, 2):
            rcopy(here, here, as_.at[half, n], ar.at[half, n], xdev(n)).start()
        rcopy(here, here, bs.at[half, 0], br.at[half, 0], other).start()

    def pass_on(half):
        for n in (1, 3, 2):
            there = shard(half, lax.rem(x + 4 - n, 4), core)
            rcopy(there, there, as_.at[half, n], ar.at[half, n], other).wait_recv()
            rcopy(there, there, bs.at[half, n], br.at[half, n], other).start()

    def gathered(half):
        for n in range(4):
            there = shard(half, lax.rem(x + 4 - n, 4), 1 - core)
            rcopy(there, there, bs.at[half, n], br.at[half, n], other).wait_recv()

    lax.fori_loop(0, EARLY, score, 0, unroll=3)
    mfin[0] = row_max(beta + 1)
    mfin[1] = row_max(EARLY)
    lax.fori_loop(0, EARLY, weigh, 0, unroll=3)
    finish(0, normal(beta + 1))
    ring_step(3, 0)

    def late_score(i, carry):
        t = EARLY + i
        s = nt(qs[1 - low_at], keys_of(t))
        room = high * BLOCK - chunk_of(t) * 256
        s = jnp.where(ahead <= room, s, NEG)
        sbuf[i] = s
        mrun[t + 1] = jnp.maximum(mrun[t], fold(s))
        return carry

    lax.fori_loop(0, LATE, late_score, 0, unroll=2)
    mfin[0] = row_max(EARLY + LATE)
    again = jnp.exp2(mfin[1] - mfin[0])
    lrun[EARLY] = lrun[EARLY] * again
    acc[EARLY] = acc[EARLY] * jnp.concatenate([again] * 4, axis=1)
    ring_step(3, 1)

    def late_weigh(i, carry):
        m = mfin[0]
        total, w = weights(sbuf[2 * i], m)
        total2, w2 = weights(sbuf[2 * i + 1], m)
        lrun[EARLY] = lrun[EARLY] + (total + total2)
        v = jnp.concatenate([values_of(EARLY + 2 * i), values_of(EARLY + 2 * i + 1)], axis=0)
        acc[EARLY] = acc[EARLY] + jnp.dot(
            jnp.concatenate([w, w2], axis=1), v, preferred_element_type=jnp.float32
        )
        return carry

    lax.fori_loop(0, LATE // 2, late_weigh, 0, unroll=2)
    finish(1, normal(EARLY))
    pass_on(0)
    ring_step(4, 0)

    def product(half, j):
        if True:
            total = nt(wbuf[j, 0], att[half, 0].reshape(256, 1024)) + nt(
                wbuf[j, 1], att[half, 1].reshape(256, 1024)
            )
            total = total.astype(jnp.bfloat16)
            for n in range(4):
                lanes = total[:, n * BLOCK : (n + 1) * BLOCK]
                csend[half, j * 4 + n] = jnp.concatenate([lanes[:112], lanes[112:]], axis=1)
            for n in range(4):
                to_x = (n // 2) * 2 + core
                local = jnp.logical_and(jnp.logical_and(to_x == x, core == n % 2), j == y)

                @pl.when(local)
                def _():
                    pltpu.make_async_copy(
                        csend.at[half, j * 4 + n], crecv.at[half, y * 4 + x], cr.at[half]
                    ).start()

                @pl.when(jnp.logical_not(local))
                def _():
                    rcopy(
                        csend.at[half, j * 4 + n], crecv.at[half, y * 4 + x], cs.at[half],
                        cr.at[half], dev(z, to_x, j, n % 2),
                    ).start()

    def project(half, zsrc):
        @pl.when(core == zsrc // 4)
        def _():
            product(half, lax.rem(zsrc, 4))

    def both(s, carry):
        project(0, lax.rem(z + 8 - s, 8))
        project(0, lax.rem(z + s, 8))
        return carry

    gathered(0)
    project(0, z)
    lax.fori_loop(1, 4, both, 0)
    ring_step(4, 1)
    project(0, lax.rem(z + 4, 8))
    pass_on(1)
    gathered(1)

    def by_distance(i, carry):
        product(1, lax.rem(y + 2 + jnp.where(i == 0, 0, jnp.where(i == 3, 2, 2 * i - 3)), 4))
        return carry

    lax.fori_loop(0, 4, by_distance, 0)

    for part, sem in (
        (lat.at[pl.ds(0, 7), 0], zs.at[0]),
        (lat.at[pl.ds(0, 3), pl.ds(0, 8)], xs.at[0]),
        (lat.at[pl.ds(0, 2)], ys.at[0]),
        (lat.at[pl.ds(0, 4)], ks.at[0]),
    ):
        rcopy(part, part, sem, kr.at[0], other).wait_send()

    @pl.when(jnp.logical_not(at_home))
    def _():
        rcopy(w_hbm, wbuf.at[wj, xl], w0.at[0], wr.at[wj, xl], other).wait_send()

    for q in range(2):
        part = xl if q == 0 else 1 - xl

        @pl.when(core == keeper)
        def _():
            for n in range(2):
                slot = wbuf.at[wj, part]
                rcopy(slot, slot, ws.at[n, wj, part], wr.at[wj, part], other).wait_send()

        for s in range(1, 4):
            for up, part, zsrc, reach in ring_moves(s, q):
                j = lax.rem(zsrc, 4)

                @pl.when(jnp.logical_and(core == zsrc // 4, s < reach))
                def _():
                    slot = wbuf.at[j, part]
                    rcopy(
                        slot, slot, ws.at[0 if up else 1, j, part], wr.at[j, part], other
                    ).wait_send()

    halves = []
    for half in range(2):
        columns = []
        rcopy(crecv.at[half], crecv.at[half], cs.at[half], cr.at[half], other).wait_recv()
        for n in range(4):
            total = None
            for m in range(4):
                term = crecv[half, m * 4 + n].astype(jnp.float32)
                total = term if total is None else total + term
            columns += [total[:, :BLOCK], total[:, BLOCK:]]
        halves.append(jnp.concatenate(columns, axis=0))
    first = jnp.where(low_at == 0, halves[0], halves[1])
    second = jnp.where(low_at == 0, halves[1], halves[0])
    mixed = jnp.concatenate([first, second], axis=1)
    out_ref[...] = jnp.transpose(mixed, (1, 0)).astype(jnp.bfloat16)
    for half in range(2):
        here = shard(half, x, core)
        for n in range(4):
            if n:
                rcopy(here, here, as_.at[half, n], ar.at[half, n], other).wait_send()
            rcopy(here, here, bs.at[half, n], br.at[half, n], other).wait_send()

        @pl.when(core == xl)
        def _():
            most = csend.at[half, pl.ds(0, 15)]
            rcopy(most, most, cs.at[half], cr.at[half], other).wait_send()

        @pl.when(core != xl)
        def _():
            rcopy(csend.at[half], csend.at[half], cs.at[half], cr.at[half], other).wait_send()


def body(queries, latent_rope, key_up, value_up, out_weight, plan):
    vm = pl.BlockSpec(memory_space=pltpu.VMEM)
    sm = pl.BlockSpec(memory_space=pltpu.SMEM)
    anywhere = pl.BlockSpec(memory_space=pl.ANY)
    bf, f32 = jnp.bfloat16, jnp.float32
    dma = pltpu.SemaphoreType.DMA
    return pl.pallas_call(
        kernel,
        out_shape=jax.ShapeDtypeStruct((128, 896), bf),
        in_specs=[sm, anywhere, anywhere, anywhere, anywhere, anywhere],
        out_specs=vm,
        scratch_shapes=[
            pltpu.SMEM((32,), jnp.int32),
            pltpu.VMEM((LATENT + ROPE, 128), bf),
            pltpu.VMEM((8, 16, PIECE, 128), bf),
            pltpu.VMEM((128, 1536), bf),
            pltpu.VMEM((512, 1024), bf),
            pltpu.VMEM((512, 1024), bf),
            pltpu.VMEM((2, ROWS, WIDE), bf),
            pltpu.VMEM((EARLY, ROWS, 256), f32),
            pltpu.VMEM((EARLY + LATE + 1, ROWS, 128), f32),
            pltpu.VMEM((2, ROWS, 128), f32),
            pltpu.VMEM((EARLY + 1, ROWS, 128), f32),
            pltpu.VMEM((EARLY + 1, ROWS, LATENT), f32),
            pltpu.VMEM((4, 2, 224, 1024), bf),
            pltpu.VMEM((2, 2, 2, 2, BLOCK, 1024), bf),
            pltpu.VMEM((2, 16, 112, 128), bf),
            pltpu.VMEM((2, 16, 112, 128), bf),
            dma((4,)), dma((1,)), dma((8,)), dma((1,)), dma((4, 8)), dma((1,)), dma((4, 8)),
            dma((1,)), dma((1,)), dma((1,)), dma((2, 4, 2)), dma((4, 2)),
            dma((2, 4)), dma((2, 4)), dma((2, 4)), dma((2, 4)), dma((2,)), dma((2,)),
        ],
        compiler_params=pltpu.CompilerParams(
            collective_id=0, has_side_effects=True, vmem_limit_bytes=56 * 2**20
        ),
    )(plan.T, latent_rope.T, queries, key_up, value_up, out_weight.T)


def solution(mesh):
    placed = (
        P("ctx", "head"),
        P("ctx", None),
        P(None, "head"),
        P(None, "head"),
        P("head", "ctx"),
        P(),
    )
    return jax.shard_map(
        body, mesh=mesh, in_specs=placed, out_specs=P("ctx", "head"), check_vma=False
    )
```

time: 84 us -> 74.5 us (0.89)
  the two profiles are of different devices: /device:TPU:7 before, /device:TPU:1 now
where the time goes in v3:
time: 74.5 us; the launch traced here: 74.3 us
  Pallas kernels  72.6 us (97%)
  local copies, waits for them, and re-layouts  1.65 us (2%)
    pallas_call x1, Pallas kernels, body(): pl.pallas_call(kernel, out_shape=jax.ShapeDtypeStruct((128, 896), bf), in...  72.6 us
    unnamed x1, local copies, waits for them, and re-layouts  1.65 us

profile of v3, /device:TPU:1, one launch (start us, length us, event | category | flops | bytes accessed | tf_op | source)
XLA Modules:
  0.0 74.3 jit_solution(9554639912509349310)
XLA Ops:
  0.0 72.6 %shard_map.64 = bf16[128,896]{1,0:T(8,128)(2,1)} custom-call(s32[2,32]{1,0:T(2,128)} %bitcast.5, bf16[576,128]{1,0:T(8,128)(2,1)} %bitcast.4, bf16[128,1536]{1,0:T(8,128)(2,1)} %q_hbm.1, bf16[512,1024]{1,0:T(8,128)(2,1)} %ku_hbm.1, bf16[512,1024]{1,0:T(8,128)(2,1)} %vu_hbm.1, bf16[224,1024]{1,0:T(8,128)(2,1)} %bitcast.3), custom_call_target="tpu_custom_call" | custom-call | tf_op jit(solution)/shard_map/pallas_call | solution.py:534
  72.6 1.6 %copy.8 = bf16[128,896]{1,0:T(8,128)(2,1)} copy(bf16[128,896]{1,0:T(8,128)(2,1)} %shard_map.64) | data formatting | bytes 458752

commit v4 on v3

--- a/solution.py
+++ b/solution.py
@@ -27,8 +27,8 @@
 
 def kernel(
     plan_ref, lrt_hbm, q_hbm, ku_hbm, vu_hbm, w_hbm, out_ref,
-    place, lrt, lat, qv, kuv, vuv, qs, sbuf, mrun, mfin, lrun, acc, wbuf, att, csend, crecv,
-    ls, zs, zr, xs, xr, ys, yr, ks, kr, w0, ws, wr, as_, ar, bs, br, cs, cr,
+    place, lrt, lat, qv, kuv, vuv, qs, sbuf, mrun, mfin, lrun, acc, wbuf, att, csend, crecv, fsend, frecv,
+    ls, zs, zr, xs, xr, ys, yr, ks, kr, w0, ws, wr, as_, ar, bs, br, cs, cr, fs, fr,
 ):
     ctx = lax.axis_index("ctx")
     head = lax.axis_index("head")
@@ -268,8 +268,9 @@
     high = jnp.maximum(p0, p1)
     low_at = jnp.where(p0 < p1, 0, 1)
     beta = lax.div(low, 4)
-    row_of = lax.broadcasted_iota(jnp.int32, (ROWS, 256), 0) % BLOCK
-    ahead = lax.broadcasted_iota(jnp.int32, (ROWS, 256), 1) - row_of
+    ahead = lax.broadcasted_iota(jnp.int32, (BLOCK, 256), 1) - lax.broadcasted_iota(
+        jnp.int32, (BLOCK, 256), 0
+    )
     left = lax.broadcasted_iota(jnp.int32, (16, 128), 1) < 64
     none = jnp.zeros((16, 128), jnp.bfloat16)
 
@@ -306,6 +307,10 @@
     def values_of(t):
         return wide_of(pieces_of(t))
 
+    def masked(s, first_row, first_key):
+        allowed = (ahead <= first_row - first_key)[None]
+        return jnp.where(allowed, s.reshape(HEAD_LOCAL, BLOCK, 256), NEG).reshape(ROWS, 256)
+
     def fold(s):
         return jnp.maximum(s[:, :128], s[:, 128:])
 
@@ -317,8 +322,7 @@
         is_low = t <= beta
         q = qs[jnp.where(is_low, low_at, 1 - low_at)]
         s = nt(q, keys_of(t))
-        room = jnp.where(is_low, low, high) * BLOCK - chunk_of(t) * 256
-        s = jnp.where(ahead <= room, s, NEG)
+        s = masked(s, jnp.where(is_low, low, high) * BLOCK, chunk_of(t) * 256)
         sbuf[t] = s
         before = jnp.where(t == beta + 1, NEG, mrun[t])
         mrun[t + 1] = jnp.maximum(before, fold(s))
@@ -346,7 +350,7 @@
         return (acc[at] / total).astype(jnp.bfloat16)
 
     def shard(half, src_x, c_):
-        return att.at[half, lax.rem(src_x, 2), src_x // 2, c_]
+        return att.at[half, lax.rem(src_x, 2) * 4 + (src_x // 2) * 2 + c_]
 
     def finish(half, o):
         for h in range(HEAD_LOCAL):
@@ -355,22 +359,21 @@
                 vuv[:, h * VDIM : (h + 1) * VDIM],
                 preferred_element_type=jnp.float32,
             )
-            att[half, xl, xh, core, :, h * VDIM : (h + 1) * VDIM] = up.astype(jnp.bfloat16)
+            att[half, xl * 4 + xh * 2 + core, :, h * VDIM : (h + 1) * VDIM] = up.astype(jnp.bfloat16)
         here = shard(half, x, core)
-        for n in (1, 3, 2):
-            rcopy(here, here, as_.at[half, n], ar.at[half, n], xdev(n)).start()
-        rcopy(here, here, bs.at[half, 0], br.at[half, 0], other).start()
+        for n in (2, 1, 3):
+            rcopy(here, here, as_.at[half], ar.at[half, n], xdev(n)).start()
+        rcopy(here, here, bs.at[half], br.at[half], other).start()
 
     def pass_on(half):
         for n in (1, 3, 2):
             there = shard(half, lax.rem(x + 4 - n, 4), core)
-            rcopy(there, there, as_.at[half, n], ar.at[half, n], other).wait_recv()
-            rcopy(there, there, bs.at[half, n], br.at[half, n], other).start()
+            rcopy(there, there, as_.at[half], ar.at[half, n], other).wait_recv()
+            rcopy(there, there, bs.at[half], br.at[half], other).start()
 
     def gathered(half):
-        for n in range(4):
-            there = shard(half, lax.rem(x + 4 - n, 4), 1 - core)
-            rcopy(there, there, bs.at[half, n], br.at[half, n], other).wait_recv()
+        four = att.at[half, pl.ds(0, 4)]
+        rcopy(four, four, bs.at[half], br.at[half], other).wait_recv()
 
     lax.fori_loop(0, EARLY, score, 0, unroll=3)
     mfin[0] = row_max(beta + 1)
@@ -379,16 +382,18 @@
     finish(0, normal(beta + 1))
     ring_step(3, 0)
 
-    def late_score(i, carry):
+    def late_score(i, carry, last=False):
         t = EARLY + i
         s = nt(qs[1 - low_at], keys_of(t))
-        room = high * BLOCK - chunk_of(t) * 256
-        s = jnp.where(ahead <= room, s, NEG)
+        if last:
+            s = masked(s, high * BLOCK, chunk_of(t) * 256)
         sbuf[i] = s
         mrun[t + 1] = jnp.maximum(mrun[t], fold(s))
         return carry
 
-    lax.fori_loop(0, LATE, late_score, 0, unroll=2)
+    lax.fori_loop(0, LATE - 2, late_score, 0, unroll=3)
+    late_score(LATE - 2, 0)
+    late_score(LATE - 1, 0, last=True)
     mfin[0] = row_max(EARLY + LATE)
     again = jnp.exp2(mfin[1] - mfin[0])
     lrun[EARLY] = lrun[EARLY] * again
@@ -409,57 +414,69 @@
     lax.fori_loop(0, LATE // 2, late_weigh, 0, unroll=2)
     finish(1, normal(EARLY))
     pass_on(0)
+
+    def pack(half, j, total):
+        total = total.astype(jnp.bfloat16)
+        for n in range(4):
+            lanes = total[:, n * BLOCK : (n + 1) * BLOCK]
+            csend[half, j * 4 + n] = jnp.concatenate([lanes[:112], lanes[112:]], axis=1)
+
+    def rows_of(half, part):
+        return att[half, part * 4 : part * 4 + 4].reshape(256, 1024)
+
+    def project(zsrc):
+        @pl.when(core == zsrc // 4)
+        def _():
+            j = lax.rem(zsrc, 4)
+            pack(0, j, nt(wbuf[j, 0], rows_of(0, 0)) + nt(wbuf[j, 1], rows_of(0, 1)))
+
+            @pl.when(j != y)
+            def _():
+                rcopy(
+                    csend.at[0, pl.ds(4 * j, 4)], crecv.at[0, pl.ds(4 * lax.rem(j + 4 - y, 4), 4)],
+                    cs.at[0], cr.at[0], dev(z, x, j, core),
+                ).start()
+
+    def both(s, carry):
+        project(lax.rem(z + 8 - s, 8))
+        project(lax.rem(z + s, 8))
+        return carry
+
+    gathered(0)
+    project(z)
+    lax.fori_loop(1, 4, both, 0)
     ring_step(4, 0)
-
-    def product(half, j):
-        if True:
-            total = nt(wbuf[j, 0], att[half, 0].reshape(256, 1024)) + nt(
-                wbuf[j, 1], att[half, 1].reshape(256, 1024)
-            )
-            total = total.astype(jnp.bfloat16)
-            for n in range(4):
-                lanes = total[:, n * BLOCK : (n + 1) * BLOCK]
-                csend[half, j * 4 + n] = jnp.concatenate([lanes[:112], lanes[112:]], axis=1)
-            for n in range(4):
-                to_x = (n // 2) * 2 + core
-                local = jnp.logical_and(jnp.logical_and(to_x == x, core == n % 2), j == y)
-
-                @pl.when(local)
-                def _():
-                    pltpu.make_async_copy(
-                        csend.at[half, j * 4 + n], crecv.at[half, y * 4 + x], cr.at[half]
-                    ).start()
-
-                @pl.when(jnp.logical_not(local))
-                def _():
-                    rcopy(
-                        csend.at[half, j * 4 + n], crecv.at[half, y * 4 + x], cs.at[half],
-                        cr.at[half], dev(z, to_x, j, n % 2),
-                    ).start()
-
-    def project(half, zsrc):
-        @pl.when(core == zsrc // 4)
-        def _():
-            product(half, lax.rem(zsrc, 4))
-
-    def both(s, carry):
-        project(0, lax.rem(z + 8 - s, 8))
-        project(0, lax.rem(z + s, 8))
-        return carry
-
-    gathered(0)
-    project(0, z)
-    lax.fori_loop(1, 4, both, 0)
     ring_step(4, 1)
-    project(0, lax.rem(z + 4, 8))
+    project(lax.rem(z + 4, 8))
     pass_on(1)
     gathered(1)
 
-    def by_distance(i, carry):
-        product(1, lax.rem(y + 2 + jnp.where(i == 0, 0, jnp.where(i == 3, 2, 2 * i - 3)), 4))
-        return carry
-
-    lax.fori_loop(0, 4, by_distance, 0)
+    def deliver(i, carry):
+        j = lax.rem(y + 2 + jnp.where(i == 0, 0, jnp.where(i == 3, 2, 2 * i - 3)), 4)
+        for n in range(4):
+            to_x = (n // 2) * 2 + core
+            local = jnp.logical_and(jnp.logical_and(to_x == x, core == n % 2), j == y)
+
+            @pl.when(local)
+            def _():
+                pltpu.make_async_copy(
+                    csend.at[1, j * 4 + n], crecv.at[1, y * 4 + x], cr.at[1]
+                ).start()
+
+            @pl.when(jnp.logical_not(local))
+            def _():
+                rcopy(
+                    csend.at[1, j * 4 + n], crecv.at[1, y * 4 + x], cs.at[1],
+                    cr.at[1], dev(z, to_x, j, n % 2),
+                ).start()
+        return carry
+
+    total = nt(wbuf[:, 0].reshape(896, 1024), rows_of(1, 0)) + nt(
+        wbuf[:, 1].reshape(896, 1024), rows_of(1, 1)
+    )
+    for j in range(4):
+        pack(1, j, total[j * 224 : (j + 1) * 224])
+    lax.fori_loop(0, 4, deliver, 0)
 
     for part, sem in (
         (lat.at[pl.ds(0, 7), 0], zs.at[0]),
@@ -493,36 +510,58 @@
                         slot, slot, ws.at[0 if up else 1, j, part], wr.at[j, part], other
                     ).wait_send()
 
-    halves = []
-    for half in range(2):
-        columns = []
-        rcopy(crecv.at[half], crecv.at[half], cs.at[half], cr.at[half], other).wait_recv()
-        for n in range(4):
-            total = None
-            for m in range(4):
-                term = crecv[half, m * 4 + n].astype(jnp.float32)
-                total = term if total is None else total + term
-            columns += [total[:, :BLOCK], total[:, BLOCK:]]
-        halves.append(jnp.concatenate(columns, axis=0))
+    three = crecv.at[0, pl.ds(4, 12)]
+    rcopy(three, three, cs.at[0], cr.at[0], other).wait_recv()
+    total = csend[0, pl.ds(4 * y, 4)].astype(jnp.float32)
+    for o in range(1, 4):
+        total = total + crecv[0, 4 * o : 4 * o + 4].astype(jnp.float32)
+    fsend[...] = total.astype(jnp.bfloat16)
+    for n in range(4):
+        to_x = (n // 2) * 2 + core
+        local = jnp.logical_and(to_x == x, core == n % 2)
+
+        @pl.when(local)
+        def _():
+            pltpu.make_async_copy(fsend.at[n], frecv.at[x], fr.at[0]).start()
+
+        @pl.when(jnp.logical_not(local))
+        def _():
+            rcopy(
+                fsend.at[n], frecv.at[x], fs.at[0], fr.at[0], dev(z, to_x, y, n % 2)
+            ).start()
+
+    rcopy(frecv, frecv, fs.at[0], fr.at[0], other).wait_recv()
+    rcopy(crecv.at[1], crecv.at[1], cs.at[1], cr.at[1], other).wait_recv()
+    columns = [[], []]
+    for n in range(4):
+        total = crecv[1, n].astype(jnp.float32)
+        for m in range(1, 4):
+            total = total + crecv[1, m * 4 + n].astype(jnp.float32)
+        for half, part in ((0, frecv[n].astype(jnp.float32)), (1, total)):
+            columns[half] += [part[:, :BLOCK], part[:, BLOCK:]]
+    halves = [jnp.concatenate(c, axis=0) for c in columns]
     first = jnp.where(low_at == 0, halves[0], halves[1])
     second = jnp.where(low_at == 0, halves[1], halves[0])
     mixed = jnp.concatenate([first, second], axis=1)
     out_ref[...] = jnp.transpose(mixed, (1, 0)).astype(jnp.bfloat16)
+
     for half in range(2):
-        here = shard(half, x, core)
-        for n in range(4):
-            if n:
-                rcopy(here, here, as_.at[half, n], ar.at[half, n], other).wait_send()
-            rcopy(here, here, bs.at[half, n], br.at[half, n], other).wait_send()
-
-        @pl.when(core == xl)
-        def _():
-            most = csend.at[half, pl.ds(0, 15)]
-            rcopy(most, most, cs.at[half], cr.at[half], other).wait_send()
-
-        @pl.when(core != xl)
-        def _():
-            rcopy(csend.at[half], csend.at[half], cs.at[half], cr.at[half], other).wait_send()
+        for count, sem in ((3, as_.at[half]), (4, bs.at[half])):
+            some = att.at[half, pl.ds(0, count)]
+            rcopy(some, some, sem, br.at[half], other).wait_send()
+    rcopy(three, three, cs.at[0], cr.at[0], other).wait_send()
+
+    @pl.when(core == xl)
+    def _():
+        home = fsend.at[pl.ds(0, 3)]
+        rcopy(home, home, fs.at[0], fr.at[0], other).wait_send()
+        sent = csend.at[1, pl.ds(0, 15)]
+        rcopy(sent, sent, cs.at[1], cr.at[1], other).wait_send()
+
+    @pl.when(core != xl)
+    def _():
+        rcopy(fsend, fsend, fs.at[0], fr.at[0], other).wait_send()
+        rcopy(csend.at[1], csend.at[1], cs.at[1], cr.at[1], other).wait_send()
 
 
 def body(queries, latent_rope, key_up, value_up, out_weight, plan):
@@ -550,12 +589,14 @@
             pltpu.VMEM((EARLY + 1, ROWS, 128), f32),
             pltpu.VMEM((EARLY + 1, ROWS, LATENT), f32),
             pltpu.VMEM((4, 2, 224, 1024), bf),
-            pltpu.VMEM((2, 2, 2, 2, BLOCK, 1024), bf),
+            pltpu.VMEM((2, 8, BLOCK, 1024), bf),
             pltpu.VMEM((2, 16, 112, 128), bf),
             pltpu.VMEM((2, 16, 112, 128), bf),
+            pltpu.VMEM((4, 112, 128), bf),
+            pltpu.VMEM((4, 112, 128), bf),
             dma((4,)), dma((1,)), dma((8,)), dma((1,)), dma((4, 8)), dma((1,)), dma((4, 8)),
             dma((1,)), dma((1,)), dma((1,)), dma((2, 4, 2)), dma((4, 2)),
-            dma((2, 4)), dma((2, 4)), dma((2, 4)), dma((2, 4)), dma((2,)), dma((2,)),
+            dma((2,)), dma((2, 4)), dma((2,)), dma((2,)), dma((2,)), dma((2,)), dma((1,)), dma((1,)),
         ],
         compiler_params=pltpu.CompilerParams(
             collective_id=0, has_side_effects=True, vmem_limit_bytes=56 * 2**20

time: 74.5 us -> 73.7 us (0.989)
  no operation moved by 1% of the time
where the time goes in v4:
time: 73.7 us; the launch traced here: 73.6 us
  Pallas kernels  71.9 us (98%)
  local copies, waits for them, and re-layouts  1.65 us (2%)
    pallas_call x1, Pallas kernels, body(): pl.pallas_call(kernel, out_shape=jax.ShapeDtypeStruct((128, 896), bf), in...  71.9 us
    unnamed x1, local copies, waits for them, and re-layouts  1.65 us

profile of v4, /device:TPU:1, one launch (start us, length us, event | category | flops | bytes accessed | tf_op | source)
XLA Modules:
  0.0 73.6 jit_solution(5035149612558589550)
XLA Ops:
  0.0 71.9 %shard_map.64 = bf16[128,896]{1,0:T(8,128)(2,1)} custom-call(s32[2,32]{1,0:T(2,128)} %bitcast.5, bf16[576,128]{1,0:T(8,128)(2,1)} %bitcast.4, bf16[128,1536]{1,0:T(8,128)(2,1)} %q_hbm.1, bf16[512,1024]{1,0:T(8,128)(2,1)} %ku_hbm.1, bf16[512,1024]{1,0:T(8,128)(2,1)} %vu_hbm.1, bf16[224,1024]{1,0:T(8,128)(2,1)} %bitcast.3), custom_call_target="tpu_custom_call" | custom-call | tf_op jit(solution)/shard_map/pallas_call | solution.py:573
  71.9 1.6 %copy.8 = bf16[128,896]{1,0:T(8,128)(2,1)} copy(bf16[128,896]{1,0:T(8,128)(2,1)} %shard_map.64) | data formatting | bytes 458752

commit v5 on v4

--- a/solution.py
+++ b/solution.py
@@ -26,8 +26,8 @@
 
 
 def kernel(
-    plan_ref, lrt_hbm, q_hbm, ku_hbm, vu_hbm, w_hbm, out_ref,
-    place, lrt, lat, qv, kuv, vuv, qs, sbuf, mrun, mfin, lrun, acc, wbuf, att, csend, crecv, fsend, frecv,
+    plan_hbm, lrt_hbm, q_hbm, ku_hbm, vu_hbm, w_hbm, out_ref,
+    plan_ref, place, lrt, lat, qv, kuv, vuv, qs, sbuf, mrun, mfin, lrun, acc, wbuf, att, csend, crecv, fsend, frecv,
     ls, zs, zr, xs, xr, ys, yr, ks, kr, w0, ws, wr, as_, ar, bs, br, cs, cr, fs, fr,
 ):
     ctx = lax.axis_index("ctx")
@@ -64,6 +64,7 @@
         pltpu.make_async_copy(q_hbm, qv, ls.at[0]),
         pltpu.make_async_copy(ku_hbm, kuv, ls.at[1]),
         pltpu.make_async_copy(vu_hbm, vuv, ls.at[2]),
+        pltpu.make_async_copy(plan_hbm, plan_ref, ls.at[4]),
     ]
     for cp in loads:
         cp.start()
@@ -196,9 +197,10 @@
         place[b] = found
         return carry
 
+    loads[4].wait()
     lax.fori_loop(0, 32, place_of, 0)
 
-    for cp in loads[1:]:
+    for cp in loads[1:4]:
         cp.wait()
     for h in range(HEAD_LOCAL):
         lo = h * (NOPE + ROPE)
@@ -398,7 +400,6 @@
     again = jnp.exp2(mfin[1] - mfin[0])
     lrun[EARLY] = lrun[EARLY] * again
     acc[EARLY] = acc[EARLY] * jnp.concatenate([again] * 4, axis=1)
-    ring_step(3, 1)
 
     def late_weigh(i, carry):
         m = mfin[0]
@@ -412,6 +413,7 @@
         return carry
 
     lax.fori_loop(0, LATE // 2, late_weigh, 0, unroll=2)
+    ring_step(3, 1)
     finish(1, normal(EARLY))
     pass_on(0)
 
@@ -566,16 +568,16 @@
 
 def body(queries, latent_rope, key_up, value_up, out_weight, plan):
     vm = pl.BlockSpec(memory_space=pltpu.VMEM)
-    sm = pl.BlockSpec(memory_space=pltpu.SMEM)
     anywhere = pl.BlockSpec(memory_space=pl.ANY)
     bf, f32 = jnp.bfloat16, jnp.float32
     dma = pltpu.SemaphoreType.DMA
     return pl.pallas_call(
         kernel,
         out_shape=jax.ShapeDtypeStruct((128, 896), bf),
-        in_specs=[sm, anywhere, anywhere, anywhere, anywhere, anywhere],
+        in_specs=[anywhere, anywhere, anywhere, anywhere, anywhere, anywhere],
         out_specs=vm,
         scratch_shapes=[
+            pltpu.SMEM((2, 32), jnp.int32),
             pltpu.SMEM((32,), jnp.int32),
             pltpu.VMEM((LATENT + ROPE, 128), bf),
             pltpu.VMEM((8, 16, PIECE, 128), bf),
@@ -594,7 +596,7 @@
             pltpu.VMEM((2, 16, 112, 128), bf),
             pltpu.VMEM((4, 112, 128), bf),
             pltpu.VMEM((4, 112, 128), bf),
-            dma((4,)), dma((1,)), dma((8,)), dma((1,)), dma((4, 8)), dma((1,)), dma((4, 8)),
+            dma((5,)), dma((1,)), dma((8,)), dma((1,)), dma((4, 8)), dma((1,)), dma((4, 8)),
             dma((1,)), dma((1,)), dma((1,)), dma((2, 4, 2)), dma((4, 2)),
             dma((2,)), dma((2, 4)), dma((2,)), dma((2,)), dma((2,)), dma((2,)), dma((1,)), dma((1,)),
         ],

time: 73.7 us -> 73.7 us (level)
  the two profiles are of different devices: /device:TPU:1 before, /device:TPU:65 now
where the time goes in v5:
time: 73.7 us; the launch traced here: 73.6 us
  Pallas kernels  72 us (98%)
  local copies, waits for them, and re-layouts  1.65 us (2%)
    pallas_call x1, Pallas kernels, body(): pl.pallas_call(kernel, out_shape=jax.ShapeDtypeStruct((128, 896), bf), in...  72 us
    unnamed x1, local copies, waits for them, and re-layouts  1.65 us

profile of v5, /device:TPU:65, one launch (start us, length us, event | category | flops | bytes accessed | tf_op | source)
XLA Modules:
  0.0 73.6 jit_solution(2402948991599727601)
XLA Ops:
  0.0 72.0 %shard_map.64 = bf16[128,896]{1,0:T(8,128)(2,1)} custom-call(s32[2,32]{1,0:T(2,128)} %bitcast.5, bf16[576,128]{1,0:T(8,128)(2,1)} %bitcast.4, bf16[128,1536]{1,0:T(8,128)(2,1)} %q_hbm.1, bf16[512,1024]{1,0:T(8,128)(2,1)} %ku_hbm.1, bf16[512,1024]{1,0:T(8,128)(2,1)} %vu_hbm.1, bf16[224,1024]{1,0:T(8,128)(2,1)} %bitcast.3), custom_call_target="tpu_custom_call" | custom-call | tf_op jit(solution)/shard_map/pallas_call | solution.py:574
  72.0 1.6 %copy.8 = bf16[128,896]{1,0:T(8,128)(2,1)} copy(bf16[128,896]{1,0:T(8,128)(2,1)} %shard_map.64) | data formatting | bytes 458752

commit v6 on v5

--- a/solution.py
+++ b/solution.py
@@ -426,50 +426,61 @@
     def rows_of(half, part):
         return att[half, part * 4 : part * 4 + 4].reshape(256, 1024)
 
-    def project(zsrc):
-        @pl.when(core == zsrc // 4)
-        def _():
-            j = lax.rem(zsrc, 4)
-            pack(0, j, nt(wbuf[j, 0], rows_of(0, 0)) + nt(wbuf[j, 1], rows_of(0, 1)))
-
-            @pl.when(j != y)
-            def _():
-                rcopy(
-                    csend.at[0, pl.ds(4 * j, 4)], crecv.at[0, pl.ds(4 * lax.rem(j + 4 - y, 4), 4)],
-                    cs.at[0], cr.at[0], dev(z, x, j, core),
-                ).start()
-
-    def both(s, carry):
-        project(lax.rem(z + 8 - s, 8))
-        project(lax.rem(z + s, 8))
+    def project(j):
+        pack(0, j, nt(wbuf[j, 0], rows_of(0, 0)) + nt(wbuf[j, 1], rows_of(0, 1)))
+
+        @pl.when(j != y)
+        def _():
+            rcopy(
+                csend.at[0, pl.ds(4 * j, 4)], crecv.at[0, pl.ds(4 * lax.rem(j + 4 - y, 4), 4)],
+                cs.at[0], cr.at[0], dev(z, x, j, core),
+            ).start()
+
+    def by_distance(i):
+        return lax.rem(y + 2 + jnp.where(i == 0, 0, jnp.where(i == 3, 2, 2 * i - 3)), 4)
+
+    across = lax.rem(z + 4, 8)
+
+    def early_columns(i, carry):
+        j = by_distance(i)
+
+        @pl.when(4 * core + j != across)
+        def _():
+            project(j)
+
         return carry
 
     gathered(0)
-    project(z)
-    lax.fori_loop(1, 4, both, 0)
+    lax.fori_loop(0, 4, early_columns, 0)
     ring_step(4, 0)
     ring_step(4, 1)
-    project(lax.rem(z + 4, 8))
+
+    @pl.when(core == across // 4)
+    def _():
+        project(lax.rem(across, 4))
+
     pass_on(1)
     gathered(1)
 
     def deliver(i, carry):
-        j = lax.rem(y + 2 + jnp.where(i == 0, 0, jnp.where(i == 3, 2, 2 * i - 3)), 4)
+        j = by_distance(i)
         for n in range(4):
-            to_x = (n // 2) * 2 + core
-            local = jnp.logical_and(jnp.logical_and(to_x == x, core == n % 2), j == y)
+            at = lax.rem(n + 2 - 2 * xh, 4)
+            to_x = (at // 2) * 2 + core
+            to_core = lax.rem(at, 2)
+            local = jnp.logical_and(jnp.logical_and(to_x == x, core == to_core), j == y)
 
             @pl.when(local)
             def _():
                 pltpu.make_async_copy(
-                    csend.at[1, j * 4 + n], crecv.at[1, y * 4 + x], cr.at[1]
+                    csend.at[1, j * 4 + at], crecv.at[1, y * 4 + x], cr.at[1]
                 ).start()
 
             @pl.when(jnp.logical_not(local))
             def _():
                 rcopy(
-                    csend.at[1, j * 4 + n], crecv.at[1, y * 4 + x], cs.at[1],
-                    cr.at[1], dev(z, to_x, j, n % 2),
+                    csend.at[1, j * 4 + at], crecv.at[1, y * 4 + x], cs.at[1],
+                    cr.at[1], dev(z, to_x, j, to_core),
                 ).start()
         return carry
 
@@ -532,20 +543,25 @@
                 fsend.at[n], frecv.at[x], fs.at[0], fr.at[0], dev(z, to_x, y, n % 2)
             ).start()
 
+    def columns_of(parts):
+        sides = []
+        for part in parts:
+            sides += [part[:, :BLOCK], part[:, BLOCK:]]
+        return jnp.concatenate(sides, axis=0)
+
     rcopy(frecv, frecv, fs.at[0], fr.at[0], other).wait_recv()
+    low_rows = columns_of([frecv[n] for n in range(4)])
     rcopy(crecv.at[1], crecv.at[1], cs.at[1], cr.at[1], other).wait_recv()
-    columns = [[], []]
+    sums = []
     for n in range(4):
         total = crecv[1, n].astype(jnp.float32)
         for m in range(1, 4):
             total = total + crecv[1, m * 4 + n].astype(jnp.float32)
-        for half, part in ((0, frecv[n].astype(jnp.float32)), (1, total)):
-            columns[half] += [part[:, :BLOCK], part[:, BLOCK:]]
-    halves = [jnp.concatenate(c, axis=0) for c in columns]
-    first = jnp.where(low_at == 0, halves[0], halves[1])
-    second = jnp.where(low_at == 0, halves[1], halves[0])
-    mixed = jnp.concatenate([first, second], axis=1)
-    out_ref[...] = jnp.transpose(mixed, (1, 0)).astype(jnp.bfloat16)
+        sums.append(total.astype(jnp.bfloat16))
+    high_rows = columns_of(sums)
+    first = jnp.where(low_at == 0, low_rows, high_rows)
+    second = jnp.where(low_at == 0, high_rows, low_rows)
+    out_ref[...] = jnp.transpose(jnp.concatenate([first, second], axis=1), (1, 0))
 
     for half in range(2):
         for count, sem in ((3, as_.at[half]), (4, bs.at[half])):

time: 73.7 us -> 74.1 us (level)
  the two profiles are of different devices: /device:TPU:65 before, /device:TPU:33 now
where the time goes in v6:
time: 74.1 us; the launch traced here: 74 us
  Pallas kernels  72.3 us (98%)
  local copies, waits for them, and re-layouts  1.65 us (2%)
    pallas_call x1, Pallas kernels, body(): pl.pallas_call(kernel, out_shape=jax.ShapeDtypeStruct((128, 896), bf), in...  72.3 us
    unnamed x1, local copies, waits for them, and re-layouts  1.65 us

profile of v6, /device:TPU:33, one launch (start us, length us, event | category | flops | bytes accessed | tf_op | source)
XLA Modules:
  0.0 74.0 jit_solution(1263661147580217619)
XLA Ops:
  0.0 72.3 %shard_map.64 = bf16[128,896]{1,0:T(8,128)(2,1)} custom-call(s32[2,32]{1,0:T(2,128)} %bitcast.5, bf16[576,128]{1,0:T(8,128)(2,1)} %bitcast.4, bf16[128,1536]{1,0:T(8,128)(2,1)} %q_hbm.1, bf16[512,1024]{1,0:T(8,128)(2,1)} %ku_hbm.1, bf16[512,1024]{1,0:T(8,128)(2,1)} %vu_hbm.1, bf16[224,1024]{1,0:T(8,128)(2,1)} %bitcast.3), custom_call_target="tpu_custom_call" | custom-call | tf_op jit(solution)/shard_map/pallas_call | solution.py:590
  72.3 1.6 %copy.8 = bf16[128,896]{1,0:T(8,128)(2,1)} copy(bf16[128,896]{1,0:T(8,128)(2,1)} %shard_map.64) | data formatting | bytes 458752

commit v7 on v6

--- a/solution.py
+++ b/solution.py
@@ -193,11 +193,12 @@
     def place_of(b, carry):
         found = jnp.int32(0)
         for c in range(32):
-            found = jnp.where(jnp.minimum(plan_ref[0, c], plan_ref[1, c]) == b, c, found)
+            found = jnp.where(lowers[c] == b, c, found)
         place[b] = found
         return carry
 
     loads[4].wait()
+    lowers = [jnp.minimum(plan_ref[0, c], plan_ref[1, c]) for c in range(32)]
     lax.fori_loop(0, 32, place_of, 0)
 
     for cp in loads[1:4]:

time: 74.1 us -> 73.7 us (level)
  no operation moved by 1% of the time
where the time goes in v7:
time: 73.7 us; the launch traced here: 73.9 us
  Pallas kernels  72.3 us (98%)
  local copies, waits for them, and re-layouts  1.65 us (2%)
    pallas_call x1, Pallas kernels, body(): pl.pallas_call(kernel, out_shape=jax.ShapeDtypeStruct((128, 896), bf), in...  72.3 us
    unnamed x1, local copies, waits for them, and re-layouts  1.65 us

profile of v7, /device:TPU:33, one launch (start us, length us, event | category | flops | bytes accessed | tf_op | source)
XLA Modules:
  0.0 73.9 jit_solution(8556953368595061073)
XLA Ops:
  0.0 72.3 %shard_map.64 = bf16[128,896]{1,0:T(8,128)(2,1)} custom-call(s32[2,32]{1,0:T(2,128)} %bitcast.5, bf16[576,128]{1,0:T(8,128)(2,1)} %bitcast.4, bf16[128,1536]{1,0:T(8,128)(2,1)} %q_hbm.1, bf16[512,1024]{1,0:T(8,128)(2,1)} %ku_hbm.1, bf16[512,1024]{1,0:T(8,128)(2,1)} %vu_hbm.1, bf16[224,1024]{1,0:T(8,128)(2,1)} %bitcast.3), custom_call_target="tpu_custom_call" | custom-call | tf_op jit(solution)/shard_map/pallas_call | solution.py:591
  72.3 1.6 %copy.8 = bf16[128,896]{1,0:T(8,128)(2,1)} copy(bf16[128,896]{1,0:T(8,128)(2,1)} %shard_map.64) | data formatting | bytes 458752
